TPU v7x, 32 devices: a whole 2x2x4 slice. The times are simulated.
32 devices in a mesh: dp: 8 (over z, y), expert: 4 (over x, core).
Axes of the slice: x: 2, y: 2, z: 4, core: 2. Of those that a mesh axis runs over, the one named last changes fastest.
Arguments:
- tokens: bfloat16 [4096, 1536], P(('dp', 'expert')), may hold values from -6 to 6
- segments: int32 [32, 128], P(('dp', 'expert')), may hold values from 0 to 3, never falling along the last dimension, each value on 1 to 64 neighbouring positions
- routes: int32 [4096, 8], P(('dp', 'expert')), may hold values from 0 to 39, all different within a row; in each aligned block of 128 rows (0 to 127, 128 to 255, ...) at most 40 rows name the same one
- w_query: bfloat16 [1536, 1536], P('dp'), may hold values from -0.15625 to 0.15625
- w_key: bfloat16 [1536, 512], P('dp'), may hold values from -0.15625 to 0.15625
- w_value: bfloat16 [1536, 512], P('dp'), may hold values from -0.15625 to 0.15625
- w_output: bfloat16 [1536, 1536], P('dp'), may hold values from -0.625 to 0.625
- w_router: bfloat16 [1536, 40], P('dp'), may hold values from -0.078125 to 0.078125
- gain_attn: bfloat16 [1536], P('dp'), may hold values from 0.099609375 to 1.8984375
- gain_moe: bfloat16 [1536], P('dp'), may hold values from 0.099609375 to 1.8984375
- w_gate_up: bfloat16 [40, 1536, 1024], P('expert'), may hold values from -0.15625 to 0.15625
- w_down: bfloat16 [40, 512, 1536], P('expert'), may hold values from -1 to 1
- cotangent: bfloat16 [4096, 1536], P(('dp', 'expert')), may hold values from -6 to 6
Outputs:
- output: bfloat16 [4096, 1536], P(('dp', 'expert'))
- grad_tokens: bfloat16 [4096, 1536], P(('dp', 'expert'))
- grad_query: float32 [1536, 1536], P('dp')
- grad_key: float32 [1536, 512], P('dp')
- grad_value: float32 [1536, 512], P('dp')
- grad_output: float32 [1536, 1536], P('dp')
- grad_router: float32 [1536, 40], P('dp')
- grad_gain_attn: float32 [1536], P('dp')
- grad_gain_moe: float32 [1536], P('dp')
- grad_gate_up: float32 [40, 1536, 1024], P('expert', 'dp')
- grad_down: float32 [40, 512, 1536], P('expert', 'dp')
Inputs may be any that keep to these rules, and one draw needn't show every extreme that they name: `routes`: in each aligned block of 128 rows (the rows of one device) no expert is named by more than 40 rows, a bound that some block reaches; the 8 experts of a row differ. `segments`: along each row the numbers never fall; a segment spans at most half of 128 positions, some segment exactly that.
All inputs are finite; a program needn't handle non-finite values.
Results may differ from a plain program's by a relative error of at most 0.023.
Values may be sent and summed in bfloat16 or wider, within the bound.
A program may use at most 256 MiB of HBM per device.

v0:
```python
import jax
import jax.numpy as jnp
from jax import lax
from jax.sharding import PartitionSpec as P

H = 24
KV = 8
HD = 64
F = 512
EXPERTS = 40
TOPK = 8
CAP = 40


epsilon = 1e-05


def tables(length, size):
    half_size = size // 2
    frequency = jnp.power(10000.0, -2.0 * jnp.arange(half_size, dtype=jnp.float32) / size)
    angles = jnp.arange(length, dtype=jnp.float32)[:, None] * frequency[None, :]
    return (jnp.cos(angles)[:, None, :], jnp.sin(angles)[:, None, :])


def rotate(source, cosine_table, sine_table):
    half_size = source.shape[-1] // 2
    first_half = source[..., :half_size]
    second_half = source[..., half_size:]
    return jnp.concatenate(
        [
            first_half * cosine_table - second_half * sine_table,
            second_half * cosine_table + first_half * sine_table,
        ],
        axis=-1,
    )


def transposed(left_side, right_side):
    return lax.dot_general(
        left_side, right_side, (((0,), (0,)), ((), ())), preferred_element_type=jnp.float32
    )


def against(left_side, right_side):
    return lax.dot_general(
        left_side, right_side, (((1,), (1,)), ((), ())), preferred_element_type=jnp.float32
    )


def local(
    tokens,
    segments,
    routes,
    w_query,
    w_key,
    w_value,
    w_output,
    w_router,
    gain_attn,
    gain_moe,
    w_gate_up,
    w_down,
    cotangent,
):
    gathered = (
        lax.all_gather(w_query, "dp", axis=0, tiled=True),
        lax.all_gather(w_key, "dp", axis=0, tiled=True),
        lax.all_gather(w_value, "dp", axis=0, tiled=True),
        lax.all_gather(w_output, "dp", axis=0, tiled=True),
        lax.all_gather(w_router, "dp", axis=0, tiled=True),
        lax.all_gather(gain_attn, "dp", axis=0, tiled=True),
        lax.all_gather(gain_moe, "dp", axis=0, tiled=True),
    )
    full_query, full_key, full_value, full_output, full_router, full_gain_attn, full_gain_moe = (
        gathered
    )
    length = tokens.shape[0]
    per_group = H // KV
    owners = lax.axis_size("expert")
    owned = w_gate_up.shape[0]
    cosine_table, sine_table = tables(length, HD)
    inputs = tokens.astype(jnp.float32)
    attn_gain = full_gain_attn.astype(jnp.float32)
    inv_attn = lax.rsqrt(jnp.mean(inputs * inputs, axis=-1, keepdims=True) + epsilon)
    unit_attn = inputs * inv_attn
    normed = (unit_attn * attn_gain).astype(jnp.bfloat16)
    queries = rotate(
        jnp.dot(normed, full_query, preferred_element_type=jnp.float32).reshape(length, H, HD),
        cosine_table,
        sine_table,
    )
    queries = queries.astype(jnp.bfloat16).reshape(length, KV, per_group, HD)
    key_rows = rotate(
        jnp.dot(normed, full_key, preferred_element_type=jnp.float32).reshape(length, KV, HD),
        cosine_table,
        sine_table,
    ).astype(jnp.bfloat16)
    values = (
        jnp.dot(normed, full_value, preferred_element_type=jnp.float32)
        .astype(jnp.bfloat16)
        .reshape(length, KV, HD)
    )
    segment = segments[0]
    position = jnp.arange(length, dtype=jnp.int32)
    allowed = (segment[:, None] == segment[None, :]) & (position[:, None] >= position[None, :])

    def score_all(query_part, key_part):
        raw_scores = (
            jnp.einsum("qkgd,skd->kgqs", query_part, key_part, preferred_element_type=jnp.float32)
            * 0.125
        )
        return jnp.where(allowed, raw_scores, -1e30)

    scores = score_all(queries, key_rows)
    maximum = jnp.max(scores, axis=-1, keepdims=True)
    lifted_scores = jnp.exp(scores - maximum)
    denominator = jnp.sum(lifted_scores, axis=-1, keepdims=True)
    logsum = maximum + jnp.log(denominator)
    attn_weights = (lifted_scores / denominator).astype(jnp.bfloat16)
    mixed = jnp.einsum("kgqs,skd->qkgd", attn_weights, values, preferred_element_type=jnp.float32)
    mixed = mixed.reshape(length, H * HD).astype(jnp.bfloat16)
    residual = inputs + jnp.dot(mixed, full_output, preferred_element_type=jnp.float32)
    moe_gain = full_gain_moe.astype(jnp.float32)
    inv_moe = lax.rsqrt(jnp.mean(residual * residual, axis=-1, keepdims=True) + epsilon)
    unit_moe = residual * inv_moe
    normed_moe = (unit_moe * moe_gain).astype(jnp.bfloat16)
    logits = jnp.dot(normed_moe, full_router, preferred_element_type=jnp.float32)
    chosen_mask = routes[:, :, None] == jnp.arange(EXPERTS, dtype=jnp.int32)
    chosen = jnp.sum(jnp.where(chosen_mask, logits[:, None, :], 0.0), axis=-1)
    largest = jnp.max(chosen, axis=-1, keepdims=True)
    lifted = jnp.exp(chosen - largest)
    gate_weights = lifted / jnp.sum(lifted, axis=-1, keepdims=True)
    one_hot = chosen_mask.reshape(length * TOPK, EXPERTS).astype(jnp.int32)
    slot_index = jnp.sum((jnp.cumsum(one_hot, axis=0) - one_hot) * one_hot, axis=-1)
    destination = routes.reshape(-1) * CAP + slot_index

    def spread(rows):
        width = rows.shape[-1]
        placed = jnp.zeros((EXPERTS * CAP, width), jnp.bfloat16).at[destination].set(rows)
        return placed.reshape(owners, owned, CAP, width)

    outgoing = spread(jnp.repeat(normed_moe, TOPK, axis=0))
    arrived = lax.all_to_all(outgoing, "expert", split_axis=0, concat_axis=0, tiled=True)
    gate_up = jnp.einsum("slcd,ldf->slcf", arrived, w_gate_up, preferred_element_type=jnp.float32)
    gate_part = gate_up[..., :F]
    up_part = gate_up[..., F:]
    activation = (gate_part * jax.nn.sigmoid(gate_part) * up_part).astype(jnp.bfloat16)
    produced = jnp.einsum(
        "slcf,lfd->slcd", activation, w_down, preferred_element_type=jnp.float32
    ).astype(jnp.bfloat16)
    returning = lax.all_to_all(produced, "expert", split_axis=0, concat_axis=0, tiled=True)
    returned, kept_gate_up, arrived = (returning, gate_up, arrived)
    picked = (
        returned.reshape(EXPERTS * CAP, -1)[destination]
        .reshape(length, TOPK, -1)
        .astype(jnp.float32)
    )
    output = (residual + jnp.sum(gate_weights[:, :, None] * picked, axis=1)).astype(jnp.bfloat16)
    gathered = (
        lax.all_gather(w_query, "dp", axis=0, tiled=True),
        lax.all_gather(w_key, "dp", axis=0, tiled=True),
        lax.all_gather(w_value, "dp", axis=0, tiled=True),
        lax.all_gather(w_output, "dp", axis=0, tiled=True),
        lax.all_gather(w_router, "dp", axis=0, tiled=True),
        lax.all_gather(gain_attn, "dp", axis=0, tiled=True),
        lax.all_gather(gain_moe, "dp", axis=0, tiled=True),
    )
    full_query, full_key, full_value, full_output, full_router, full_gain_attn, full_gain_moe = (
        gathered
    )
    attn_gain = full_gain_attn.astype(jnp.float32)
    moe_gain = full_gain_moe.astype(jnp.float32)
    grad_out = cotangent.astype(jnp.float32)
    grad_gates = jnp.sum(grad_out[:, None, :] * picked, axis=-1)
    pair_grad = (
        (gate_weights[:, :, None] * grad_out[:, None, :])
        .astype(jnp.bfloat16)
        .reshape(length * TOPK, -1)
    )
    grad_arrived = lax.all_to_all(
        spread(pair_grad), "expert", split_axis=0, concat_axis=0, tiled=True
    )
    gate_part = kept_gate_up[..., :F]
    up_part = kept_gate_up[..., F:]
    sigmoid_gate = jax.nn.sigmoid(gate_part)
    swished = gate_part * sigmoid_gate
    activation = (swished * up_part).astype(jnp.bfloat16)
    grad_act = jnp.einsum(
        "slcd,lfd->slcf", grad_arrived, w_down, preferred_element_type=jnp.float32
    )
    grad_gate_rows = jnp.concatenate(
        [
            grad_act * up_part * sigmoid_gate * (1.0 + gate_part * (1.0 - sigmoid_gate)),
            grad_act * swished,
        ],
        axis=-1,
    ).astype(jnp.bfloat16)
    grad_rows = jnp.einsum(
        "slcf,ldf->slcd", grad_gate_rows, w_gate_up, preferred_element_type=jnp.float32
    ).astype(jnp.bfloat16)
    rows_back = lax.all_to_all(grad_rows, "expert", split_axis=0, concat_axis=0, tiled=True)
    part_gate_up = jnp.einsum(
        "slcd,slcf->ldf", arrived, grad_gate_rows, preferred_element_type=jnp.float32
    )
    part_down = jnp.einsum(
        "slcf,slcd->lfd", activation, grad_arrived, preferred_element_type=jnp.float32
    )
    grad_chosen = gate_weights * (
        grad_gates - jnp.sum(gate_weights * grad_gates, axis=-1, keepdims=True)
    )
    grad_logits = jnp.sum(jnp.where(chosen_mask, grad_chosen[:, :, None], 0.0), axis=1).astype(
        jnp.bfloat16
    )
    part_router = transposed(normed_moe, grad_logits)
    returned_rows = (
        rows_back.reshape(EXPERTS * CAP, -1)[destination]
        .reshape(length, TOPK, -1)
        .astype(jnp.float32)
    )
    grad_normed_moe = jnp.sum(returned_rows, axis=1) + against(grad_logits, full_router)
    part_gain_moe = jnp.sum(grad_normed_moe * unit_moe, axis=0)
    scaled_moe = grad_normed_moe * moe_gain
    grad_residual = grad_out + inv_moe * (
        scaled_moe - unit_moe * jnp.mean(scaled_moe * unit_moe, axis=-1, keepdims=True)
    )
    grad_branch = grad_residual.astype(jnp.bfloat16)
    part_output = transposed(mixed, grad_branch)
    grad_mixed = (
        against(grad_branch, full_output).astype(jnp.bfloat16).reshape(length, KV, per_group, HD)
    )
    scores = score_all(queries, key_rows)
    full_weights = jnp.exp(scores - logsum)
    grad_weights = jnp.einsum(
        "qkgd,skd->kgqs", grad_mixed, values, preferred_element_type=jnp.float32
    )
    grad_values = jnp.einsum(
        "kgqs,qkgd->skd",
        full_weights.astype(jnp.bfloat16),
        grad_mixed,
        preferred_element_type=jnp.float32,
    )
    grad_values = grad_values.astype(jnp.bfloat16).reshape(length, KV * HD)
    grad_scores = (
        full_weights * (grad_weights - jnp.sum(full_weights * grad_weights, axis=-1, keepdims=True))
    ).astype(jnp.bfloat16)
    grad_queries = (
        jnp.einsum("kgqs,skd->qkgd", grad_scores, key_rows, preferred_element_type=jnp.float32)
        * 0.125
    )
    grad_queries = (
        rotate(grad_queries.reshape(length, H, HD), cosine_table, -sine_table)
        .astype(jnp.bfloat16)
        .reshape(length, H * HD)
    )
    grad_keys = (
        jnp.einsum("kgqs,qkgd->skd", grad_scores, queries, preferred_element_type=jnp.float32)
        * 0.125
    )
    grad_keys = (
        rotate(grad_keys, cosine_table, -sine_table).astype(jnp.bfloat16).reshape(length, KV * HD)
    )
    part_query = transposed(normed, grad_queries)
    part_key = transposed(normed, grad_keys)
    part_value = transposed(normed, grad_values)
    grad_normed = (
        against(grad_queries, full_query)
        + against(grad_keys, full_key)
        + against(grad_values, full_value)
    )
    part_gain_attn = jnp.sum(grad_normed * unit_attn, axis=0)
    scaled_attn = grad_normed * attn_gain
    grad_tokens = (
        grad_residual
        + inv_attn
        * (scaled_attn - unit_attn * jnp.mean(scaled_attn * unit_attn, axis=-1, keepdims=True))
    ).astype(jnp.bfloat16)
    summed = (
        lax.psum(part_query.astype(jnp.bfloat16), "expert").astype(jnp.float32),
        lax.psum(part_key.astype(jnp.bfloat16), "expert").astype(jnp.float32),
        lax.psum(part_value.astype(jnp.bfloat16), "expert").astype(jnp.float32),
        lax.psum(part_output.astype(jnp.bfloat16), "expert").astype(jnp.float32),
        lax.psum(part_router.astype(jnp.bfloat16), "expert").astype(jnp.float32),
        lax.psum(part_gain_attn.astype(jnp.bfloat16), "expert").astype(jnp.float32),
        lax.psum(part_gain_moe.astype(jnp.bfloat16), "expert").astype(jnp.float32),
    )
    part_query, part_key, part_value, part_output, part_router, part_gain_attn, part_gain_moe = (
        summed
    )
    scattered = (
        lax.psum_scatter(
            part_query.astype(jnp.bfloat16), "dp", scatter_dimension=0, tiled=True
        ).astype(jnp.float32),
        lax.psum_scatter(
            part_key.astype(jnp.bfloat16), "dp", scatter_dimension=0, tiled=True
        ).astype(jnp.float32),
        lax.psum_scatter(
            part_value.astype(jnp.bfloat16), "dp", scatter_dimension=0, tiled=True
        ).astype(jnp.float32),
        lax.psum_scatter(
            part_output.astype(jnp.bfloat16), "dp", scatter_dimension=0, tiled=True
        ).astype(jnp.float32),
        lax.psum_scatter(
            part_router.astype(jnp.bfloat16), "dp", scatter_dimension=0, tiled=True
        ).astype(jnp.float32),
        lax.psum_scatter(
            part_gain_attn.astype(jnp.bfloat16), "dp", scatter_dimension=0, tiled=True
        ).astype(jnp.float32),
        lax.psum_scatter(
            part_gain_moe.astype(jnp.bfloat16), "dp", scatter_dimension=0, tiled=True
        ).astype(jnp.float32),
        lax.psum_scatter(
            part_gate_up.astype(jnp.bfloat16), "dp", scatter_dimension=1, tiled=True
        ).astype(jnp.float32),
        lax.psum_scatter(
            part_down.astype(jnp.bfloat16), "dp", scatter_dimension=1, tiled=True
        ).astype(jnp.float32),
    )
    (
        shard_query,
        shard_key,
        shard_value,
        shard_output,
        shard_router,
        shard_gain_attn,
        shard_gain_moe,
        shard_gate_up,
        shard_down,
    ) = scattered
    return (
        output,
        grad_tokens,
        shard_query,
        shard_key,
        shard_value,
        shard_output,
        shard_router,
        shard_gain_attn,
        shard_gain_moe,
        shard_gate_up,
        shard_down,
    )


def solution(mesh):
    return jax.shard_map(
        local,
        mesh=mesh,
        in_specs=(
            P(("dp", "expert"), None),
            P(("dp", "expert"), None),
            P(("dp", "expert"), None),
            P("dp", None),
            P("dp", None),
            P("dp", None),
            P("dp", None),
            P("dp", None),
            P("dp"),
            P("dp"),
            P("expert", None, None),
            P("expert", None, None),
            P(("dp", "expert"), None),
        ),
        out_specs=(
            P(("dp", "expert"), None),
            P(("dp", "expert"), None),
            P("dp", None),
            P("dp", None),
            P("dp", None),
            P("dp", None),
            P("dp", None),
            P("dp"),
            P("dp"),
            P("expert", "dp", None),
            P("expert", "dp", None),
        ),
        check_vma=False,
    )
```

profile of v0, /device:TPU:0, one launch (start us, length us, event | category | flops | bytes accessed | tf_op | source)
XLA Modules:
  0.0 1788.5 jit_solution(17424768999356870738)
XLA Ops:
  14.7 23.7 %all-reduce.5 = (bf16[1536]{0:T(1024)(128)(2,1)S(1)}, bf16[1536]{0:T(1024)(128)(2,1)S(1)}) all-reduce(bf16[1536]{0:T(1024)(128)(2,1)S(1)} %dynamic-update-slice, bf16[1536]{0:T(1024)(128)(2,1)S(1)} %dynamic-update-slice.1), channel_id=1, replica_groups=mesh['dp'=8,'expert'=4] {'dp'}, use_global_device_ids=true, to_apply=%add | all-reduce | flops 3072 | bytes 12288
  39.3 11.3 reduce-window.6
  58.9 43.3 %all-gather.8.cloned.1.call-done = bf16[1536,512]{1,0:T(8,128)(2,1)} async-done(((bf16[192,512]{1,0:T(8,128)(2,1)}), bf16[1536,512]{1,0:T(8,128)(2,1)}) %all-gather.8.cloned.1.call-update) | async-done | bytes 1572880 | tf_op jit(solution)/shard_map/all_gather | solution.py:67
  104.5 78.7 %all-gather.10.cloned.1.call-done = bf16[1536,1536]{1,0:T(8,128)(2,1)} async-done(((bf16[192,1536]{1,0:T(8,128)(2,1)}), bf16[1536,1536]{1,0:T(8,128)(2,1)}) %all-gather.10.cloned.1.call-update) | async-done | bytes 4718608 | tf_op jit(solution)/shard_map/all_gather | solution.py:66
  188.9 74.4 %all-gather.12.cloned.1.call-done = bf16[1536,1536]{1,0:T(8,128)(2,1)} async-done(((bf16[192,1536]{1,0:T(8,128)(2,1)}), bf16[1536,1536]{1,0:T(8,128)(2,1)}) %all-gather.12.cloned.1.call-update) | async-done | bytes 4718608 | tf_op jit(solution)/shard_map/all_gather | solution.py:69
  280.7 30.6 %all-gather = bf16[8,192,40]{1,2,0:T(8,128)(2,1)S(1)} all-gather(bf16[1,192,40]{1,2,0:T(8,128)(2,1)S(1)} %bitcast.199), channel_id=1, replica_groups=mesh['dp'=8,'expert'=4] {'dp'}, dimensions={0}, use_global_device_ids=true | all-gather | bytes 138240 | tf_op jit(solution)/shard_map/all_gather | solution.py:70
  341.8 17.2 fusion.30
  359.0 38.8 %all-to-all-done.2 = bf16[4,10,40,1536]{3,2,1,0:T(8,128)(2,1)} async-done(((bf16[4,10,40,1536]{3,2,1,0:T(8,128)(2,1)}), bf16[4,10,40,1536]{3,2,1,0:T(8,128)(2,1)}, u32[]{:S(2)}, u32[]{:S(2)}) %all-to-all-start.2) | async-done | bytes 4915232 | tf_op jit(solution)/shard_map/all_to_all | solution.py:180
  397.8 13.1 fusion.20
  410.9 17.9 convert_bitcast_fusion
  450.3 44.6 %all-to-all-done.3 = bf16[4,10,40,1536]{3,2,1,0:T(8,128)(2,1)} async-done(((bf16[4,10,40,1536]{3,2,1,0:T(8,128)(2,1)}), bf16[4,10,40,1536]{3,2,1,0:T(8,128)(2,1)}, u32[]{:S(2)}, u32[]{:S(2)}) %all-to-all-start.3) | async-done | bytes 4915232 | tf_op jit(solution)/shard_map/all_to_all | solution.py:201
  502.7 10.4 gather_fusion.1
  518.0 37.8 %all-to-all-done.1 = bf16[4,10,40,1536]{3,2,1,0:T(8,128)(2,1)} async-done(((bf16[4,10,40,1536]{3,2,1,0:T(8,128)(2,1)}), bf16[4,10,40,1536]{3,2,1,0:T(8,128)(2,1)}, u32[]{:S(2)}, u32[]{:S(2)}) %all-to-all-start.1) | async-done | bytes 4915232 | tf_op jit(solution)/shard_map/all_to_all | solution.py:151
  555.8 10.4 gather_fusion
  599.9 47.1 %reduce-scatter.18.cloned.1.call-done = bf16[192,512]{1,0:T(8,128)(2,1)} async-done(((bf16[1536,512]{1,0:T(8,128)(2,1)}), bf16[192,512]{1,0:T(8,128)(2,1)}) %reduce-scatter.18.cloned.1.call-update) | async-done | bytes 196624 | tf_op jit(solution)/shard_map/reduce_scatter | solution.py:296
  647.0 68.1 %reduce-scatter.16.cloned.1.call-done = bf16[192,512]{1,0:T(8,128)(2,1)} async-done(((bf16[1536,512]{1,0:T(8,128)(2,1)}), bf16[192,512]{1,0:T(8,128)(2,1)}) %reduce-scatter.16.cloned.1.call-update) | async-done | bytes 196624 | tf_op jit(solution)/shard_map/reduce_scatter | solution.py:293
  715.1 97.8 %reduce-scatter.20.cloned.1.call-done = bf16[192,1536]{1,0:T(8,128)(2,1)} async-done(((bf16[1536,1536]{1,0:T(8,128)(2,1)}), bf16[192,1536]{1,0:T(8,128)(2,1)}) %reduce-scatter.20.cloned.1.call-update) | async-done | bytes 589840 | tf_op jit(solution)/shard_map/reduce_scatter | solution.py:299
  813.0 99.3 %reduce-scatter.14.cloned.1.call-done = bf16[192,1536]{1,0:T(8,128)(2,1)} async-done(((bf16[1536,1536]{1,0:T(8,128)(2,1)}), bf16[192,1536]{1,0:T(8,128)(2,1)}) %reduce-scatter.14.cloned.1.call-update) | async-done | bytes 589840 | tf_op jit(solution)/shard_map/reduce_scatter | solution.py:290
  922.6 16.6 bitcast_convert_fusion
  946.5 20.5 %all-reduce.4 = (bf16[1536]{0:T(1024)(128)(2,1)S(1)}, bf16[1536]{0:T(1024)(128)(2,1)S(1)}) all-reduce(bf16[1536]{0:T(1024)(128)(2,1)S(1)} %get-tuple-element.15, bf16[1536]{0:T(1024)(128)(2,1)S(1)} %get-tuple-element.13), channel_id=7, replica_groups=mesh['dp'=8,'expert'=4] {'dp'}, use_global_device_ids=true, to_apply=%region_32.33.clone | all-reduce | flops 3072 | bytes 12288
  978.1 10.7 all-reduce.6
  990.6 31.6 %all-reduce.10.cloned.1.call-done = (bf16[192,1536]{1,0:T(8,128)(2,1)}, bf16[192,512]{1,0:T(8,128)(2,1)}, bf16[192,512]{1,0:T(8,128)(2,1)}, bf16[192,1536]{1,0:T(8,128)(2,1)}) async-done(((bf16[192,1536]{1,0:T(8,128)(2,1)}, bf16[192,512]{1,0:T(8,128)(2,1)}, bf16[192,512]{1,0:T(8,128)(2,1)}, bf16[192,1536]{1,0:T(8,128)(2,1)}), (bf16[192,1536]{1,0:T(8,128)(2,1)}, bf16[192,512]{1,0:T(8,128)(2,1)}, ...) | async-done | bytes 1572880 | tf_op jit(solution)/shard_map/psum | solution.py:278
  1029.1 248.0 %reduce-scatter.12.cloned.1.call-done = bf16[10,64,1536]{2,1,0:T(8,128)(2,1)} async-done(((bf16[10,512,1536]{2,1,0:T(8,128)(2,1)}), bf16[10,64,1536]{2,1,0:T(8,128)(2,1)}) %reduce-scatter.12.cloned.1.call-update) | async-done | bytes 1966096 | tf_op jit(solution)/shard_map/reduce_scatter | solution.py:314
  1281.0 493.8 %reduce-scatter.10.cloned.1.call-done = bf16[10,192,1024]{2,1,0:T(8,128)(2,1)} async-done(((bf16[10,1536,1024]{2,1,0:T(8,128)(2,1)}), bf16[10,192,1024]{2,1,0:T(8,128)(2,1)}) %reduce-scatter.10.cloned.1.call-update) | async-done | bytes 3932176 | tf_op jit(solution)/shard_map/reduce_scatter | solution.py:311
  (211 shorter events, 186.0 us)
Async XLA Ops:
  7.2 49.8 %all-gather.6.cloned.1.call-start = ((), (), s32[]{:S(2)}) async-start(), calls=%async_computation.11 | async-start | bytes 1769472 | tf_op jit(solution)/shard_map/all_gather | solution.py:68
  7.9 94.3 %all-gather.8.cloned.1.call-start = ((), (), s32[]{:S(2)}) async-start(), calls=%async_computation.12 | async-start | bytes 1769472 | tf_op jit(solution)/shard_map/all_gather | solution.py:67
  8.7 174.5 %all-gather.10.cloned.1.call-start = ((), (), s32[]{:S(2)}) async-start(), calls=%async_computation.13 | async-start | bytes 5308416 | tf_op jit(solution)/shard_map/all_gather | solution.py:66
  9.4 253.8 %all-gather.12.cloned.1.call-start = ((), (), s32[]{:S(2)}) async-start(), calls=%async_computation.14 | async-start | bytes 5308416 | tf_op jit(solution)/shard_map/all_gather | solution.py:69
  38.4 228.1 %copy-start.27 = (f32[1536]{0:T(1024)}, f32[1536]{0:T(1024)S(1)}, u32[]{:S(2)}) copy-start(f32[1536]{0:T(1024)S(1)} %convert_element_type.195) | copy-start | bytes 18436
  51.3 136.1 %copy-start.33 = (f32[128]{0:T(128)}, f32[128]{0:T(128)S(1)}, u32[]{:S(2)}) copy-start(f32[128]{0:T(128)S(1)} %add_rsqrt_fusion.1) | copy-start | bytes 1540
  51.4 215.3 %copy-start.36 = (s32[1024,1]{0,1:T(1,128)}, s32[1024,1]{0,1:T(1,128)S(1)}, u32[]{:S(2)}) copy-start(s32[1024,1]{0,1:T(1,128)S(1)} %compare_select_fusion) | copy-start | bytes 12292
  52.2 135.3 %copy-start.17 = (f32[128,32]{0,1:T(8,128)}, f32[128,32]{0,1:T(8,128)S(1)}, u32[]{:S(2)}) copy-start(f32[128,32]{0,1:T(8,128)S(1)} %get-tuple-element.45) | copy-start | bytes 49156
  58.9 129.5 %copy-start.15 = (bf16[128,512]{0,1:T(8,128)(2,1)}, bf16[128,512]{0,1:T(8,128)(2,1)S(1)}, u32[]{:S(2)}) copy-start(bf16[128,512]{0,1:T(8,128)(2,1)S(1)} %copy.107) | copy-start | bytes 393220
  104.5 83.2 %copy-start.21 = (bf16[128,8,32]{0,2,1:T(8,128)(2,1)}, bf16[128,8,32]{0,2,1:T(8,128)(2,1)S(1)}, u32[]{:S(2)}) copy-start(bf16[128,8,32]{0,2,1:T(8,128)(2,1)S(1)} %get-tuple-element.39) | copy-start | bytes 196612
  104.5 83.2 %copy-start.23 = (bf16[128,8,32]{0,2,1:T(8,128)(2,1)}, bf16[128,8,32]{0,2,1:T(8,128)(2,1)S(1)}, u32[]{:S(2)}) copy-start(bf16[128,8,32]{0,2,1:T(8,128)(2,1)S(1)} %get-tuple-element.40) | copy-start | bytes 196612
  188.9 77.6 %copy-start.4 = (bf16[8,64,3,128]{3,1,2,0:T(8,128)(2,1)}, bf16[8,64,3,128]{3,1,2,0:T(8,128)(2,1)S(1)}, u32[]{:S(2)}) copy-start(bf16[8,64,3,128]{3,1,2,0:T(8,128)(2,1)S(1)} %convolution_convert_fusion.6) | copy-start | bytes 1179652
  275.7 61.0 %all-to-all-start = ((bf16[4,10,40,1536]{3,2,1,0:T(8,128)(2,1)}), bf16[4,10,40,1536]{3,2,1,0:T(8,128)(2,1)}, u32[]{:S(2)}, u32[]{:S(2)}) async-start(bf16[4,10,40,1536]{3,2,1,0:T(8,128)(2,1)} %bitcast.178), calls=%async_computation | async-start | bytes 9830400 | tf_op jit(solution)/shard_map/all_to_all | solution.py:143
  336.7 61.1 %all-to-all-start.2 = ((bf16[4,10,40,1536]{3,2,1,0:T(8,128)(2,1)}), bf16[4,10,40,1536]{3,2,1,0:T(8,128)(2,1)}, u32[]{:S(2)}, u32[]{:S(2)}) async-start(bf16[4,10,40,1536]{3,2,1,0:T(8,128)(2,1)} %bitcast.177), calls=%async_computation.2 | async-start | bytes 9830400 | tf_op jit(solution)/shard_map/all_to_all | solution.py:180
  433.9 61.0 %all-to-all-start.3 = ((bf16[4,10,40,1536]{3,2,1,0:T(8,128)(2,1)}), bf16[4,10,40,1536]{3,2,1,0:T(8,128)(2,1)}, u32[]{:S(2)}, u32[]{:S(2)}) async-start(bf16[4,10,40,1536]{3,2,1,0:T(8,128)(2,1)} %copy.122), calls=%async_computation.3 | async-start | bytes 9830400 | tf_op jit(solution)/shard_map/all_to_all | solution.py:201
  494.8 61.0 %all-to-all-start.1 = ((bf16[4,10,40,1536]{3,2,1,0:T(8,128)(2,1)}), bf16[4,10,40,1536]{3,2,1,0:T(8,128)(2,1)}, u32[]{:S(2)}, u32[]{:S(2)}) async-start(bf16[4,10,40,1536]{3,2,1,0:T(8,128)(2,1)} %copy.119), calls=%async_computation.1 | async-start | bytes 9830400 | tf_op jit(solution)/shard_map/all_to_all | solution.py:151
  499.8 147.2 %reduce-scatter.18.cloned.1.call-start = ((), (), s32[]{:S(2)}) async-start(), calls=%async_computation.19 | async-start | bytes 1769472 | tf_op jit(solution)/shard_map/reduce_scatter | solution.py:296
  584.7 130.4 %reduce-scatter.16.cloned.1.call-start = ((), (), s32[]{:S(2)}) async-start(), calls=%async_computation.18 | async-start | bytes 1769472 | tf_op jit(solution)/shard_map/reduce_scatter | solution.py:293
  588.8 224.1 %reduce-scatter.20.cloned.1.call-start = ((), (), s32[]{:S(2)}) async-start(), calls=%async_computation.20 | async-start | bytes 5308416 | tf_op jit(solution)/shard_map/reduce_scatter | solution.py:299
  592.7 319.5 %reduce-scatter.14.cloned.1.call-start = ((), (), s32[]{:S(2)}) async-start(), calls=%async_computation.17 | async-start | bytes 5308416 | tf_op jit(solution)/shard_map/reduce_scatter | solution.py:290
  597.7 379.5 %reduce-scatter.22.cloned.1.call-start = ((), (), s32[]{:S(2)}) async-start(), calls=%async_computation.21 | async-start | bytes 442368
  599.8 422.4 %all-reduce.10.cloned.1.call-start = ((), (), s32[]{:S(2)}) async-start(), calls=%async_computation.22 | async-start | bytes 3145728 | tf_op jit(solution)/shard_map/psum | solution.py:278
  912.3 364.7 %reduce-scatter.12.cloned.1.call-start = ((), (), s32[]{:S(2)}) async-start(), calls=%async_computation.16 | async-start | bytes 17694720 | tf_op jit(solution)/shard_map/reduce_scatter | solution.py:314
  922.5 852.3 %reduce-scatter.10.cloned.1.call-start = ((), (), s32[]{:S(2)}) async-start(), calls=%async_computation.15 | async-start | bytes 35389440 | tf_op jit(solution)/shard_map/reduce_scatter | solution.py:311
  (32 other events, 288.1 us)
Sparse Core Ops, SparseCore 0:
  10.2 46.6 all-gather.5
  59.1 43.0 all-gather.7
  104.4 78.6 all-gather.9
  185.2 78.0 all-gather.11
  584.8 62.1 reduce-scatter.17
  651.2 63.8 reduce-scatter.15
  718.8 94.1 reduce-scatter.19
  817.2 95.0 reduce-scatter.13
  916.1 61.1 reduce-scatter.21
  979.7 42.4 all-reduce.9
  1025.8 251.1 reduce-scatter.11
  1280.7 494.0 reduce-scatter.9
where the time goes:
time: 1800 us; the launch traced here: 1790 us
  waiting for transfers between devices  1430 us (79%)
  matrix products  123 us (7%)
  blocking collectives  85.4 us (5%)
  other arithmetic  63.3 us (4%)
  local copies, waits for them, and re-layouts  51.4 us (3%)
  starting transfers between devices  21.1 us (1%)
    reduce_scatter x1, waiting for transfers between devices, local(): lax.psum_scatter(part_gate_up.astype(jnp.bfloat16), 'dp', scatter_dimensi...  494 us
    reduce_scatter x1, waiting for transfers between devices, local(): lax.psum_scatter(part_down.astype(jnp.bfloat16), 'dp', scatter_dimension=...  248 us
    reduce_scatter x1, waiting for transfers between devices, local(): lax.psum_scatter(part_query.astype(jnp.bfloat16), 'dp', scatter_dimension...  99.3 us
    reduce_scatter x1, waiting for transfers between devices, local(): lax.psum_scatter(part_output.astype(jnp.bfloat16), 'dp', scatter_dimensio...  97.8 us
    all_gather x1, waiting for transfers between devices, local(): lax.all_gather(w_query, 'dp', axis=0, tiled=True)  78.7 us
    all_gather x1, waiting for transfers between devices, local(): lax.all_gather(w_output, 'dp', axis=0, tiled=True)  74.4 us
    reduce_scatter x1, waiting for transfers between devices, local(): lax.psum_scatter(part_key.astype(jnp.bfloat16), 'dp', scatter_dimension=0...  68.1 us
    reduce_scatter x1, waiting for transfers between devices, local(): lax.psum_scatter(part_value.astype(jnp.bfloat16), 'dp', scatter_dimension...  47.1 us
  transfers between devices with their start and end apart: 16, of which 16 were waited for; matrix products, arithmetic and copies ran while one was open for 8% of the time, Pallas kernels for 0%

commit v1 on v0

v1 whole, which is shorter than its diff:
```python
import functools

import jax
import jax.numpy as jnp
from jax import lax
from jax.experimental import pallas as pl
from jax.experimental.pallas import tpu as pltpu
from jax.sharding import PartitionSpec as P

H = 24
KV = 8
HD = 64
F = 512
EXPERTS = 40
ZLINE = 4


epsilon = 1e-05
f32 = jnp.float32
bf16 = jnp.bfloat16


def tables(length, size):
    half_size = size // 2
    frequency = jnp.power(10000.0, -2.0 * jnp.arange(half_size, dtype=f32) / size)
    angles = jnp.arange(length, dtype=f32)[:, None] * frequency[None, :]
    return (jnp.cos(angles)[:, None, :], jnp.sin(angles)[:, None, :])


def rotate(source, cosine_table, sine_table):
    half_size = source.shape[-1] // 2
    first_half = source[..., :half_size]
    second_half = source[..., half_size:]
    return jnp.concatenate(
        [
            first_half * cosine_table - second_half * sine_table,
            second_half * cosine_table + first_half * sine_table,
        ],
        axis=-1,
    )


def dot(left_side, right_side):
    return jnp.dot(left_side, right_side, preferred_element_type=f32)


def transposed(left_side, right_side):
    return lax.dot_general(
        left_side, right_side, (((0,), (0,)), ((), ())), preferred_element_type=f32
    )


def against(left_side, right_side):
    return lax.dot_general(
        left_side, right_side, (((1,), (1,)), ((), ())), preferred_element_type=f32
    )


def swap(value, axis, mask):
    size = lax.axis_size(axis)
    return lax.ppermute(value, axis, [(i, i ^ mask) for i in range(size)])


def pick(value, at):
    return lax.dynamic_index_in_dim(value, at, 0, keepdims=False)


def bits(first, size):
    masks, step = [], 1
    while step < size:
        masks.append(first * step)
        step *= 2
    return masks


class Place:
    def __init__(self):
        self.dp_size = lax.axis_size("dp")
        self.ex_size = lax.axis_size("expert")
        self.dp = lax.axis_index("dp")
        self.ex = lax.axis_index("expert")
        self.rows_y = self.dp_size // ZLINE
        self.z = self.dp // self.rows_y
        self.y = self.dp % self.rows_y
        self.z_bits = bits(self.rows_y, ZLINE)
        self.y_bits = bits(1, self.rows_y)
        self.x_bits = bits(2, self.ex_size // 2)


def gather_weights(place, shard):
    n, columns = shard.shape
    piece = n // 6
    cut = shard.reshape(3, 2, piece, columns)
    core = place.ex % 2
    side = (place.ex // 2) % 2
    own = pick(cut.swapaxes(0, 1), core)
    sibling = pick(cut.swapaxes(0, 1), 1 - core)

    def ordered(parts):
        return jnp.stack([pick(parts, 2 * side), parts[1], pick(parts, 2 - 2 * side)])

    own, sibling = ordered(own), ordered(sibling)
    blocks = {0: own[:2]}
    for mask in place.z_bits + place.y_bits:
        blocks.update({m ^ mask: swap(v, "dp", mask) for m, v in list(blocks.items())})
    rows = []
    for m in range(place.dp_size):
        if m == 0:
            rows.append(jnp.stack([own, sibling], axis=1))
            continue
        other = swap(blocks[m][0], "expert", 2)
        trio = jnp.concatenate([blocks[m], other[None]], axis=0)
        rows.append(jnp.stack([trio, swap(trio, "expert", 1)], axis=1))
    full = jnp.stack(rows)
    total = place.dp_size * n
    k = jnp.arange(total, dtype=jnp.int32)
    block, part = k // n, (k % n) // (2 * piece)
    half, line = (k % (2 * piece)) // piece, k % piece
    part = jnp.where(part == 1, 1, jnp.where(part == 0, 2 * side, 2 - 2 * side))
    at = (block ^ place.dp) * n + part * 2 * piece + (half ^ core) * piece + line
    order = (at[:, None] == jnp.arange(total, dtype=jnp.int32)[None, :]).astype(bf16)
    return full.reshape(total, columns), order


def scatter_weights(place, part):
    total, columns = part.shape
    n = total // place.dp_size
    piece = n // 6
    core = place.ex % 2
    side = (place.ex // 2) % 2

    def add(left, right):
        return (left.astype(f32) + right.astype(f32)).astype(bf16)

    part = part.reshape(place.dp_size, 3, 2, piece, columns)
    kept = add(part[:, :, 0], swap(part[:, :, 1], "expert", 1))
    first = add(kept[:, 0], swap(kept[:, 2], "expert", 2))
    blocks = {m: jnp.stack([first[m], kept[m, 1]]) for m in range(place.dp_size)}
    for mask in (place.z_bits + place.y_bits)[::-1]:
        blocks = {
            m: add(v, swap(blocks[m ^ mask], "dp", mask))
            for m, v in blocks.items()
            if m & mask == 0
        }
    mine = blocks[0]
    middle = add(mine[1], swap(mine[1], "expert", 2))
    trio = jnp.stack([mine[0], middle, swap(mine[0], "expert", 2)])
    for mask in place.x_bits[1:]:
        trio = add(trio, swap(trio, "expert", mask))
    both = jnp.stack([trio, swap(trio, "expert", 1)], axis=1)
    both = jnp.where(side == 0, both, both[::-1])
    both = jnp.where(core == 0, both, both[:, ::-1])
    return both.reshape(n, columns).astype(f32)


def gather_tokens(place, block):
    blocks = {0: block}
    for mask in place.z_bits:
        blocks.update({m ^ mask: swap(v, "dp", mask) for m, v in list(blocks.items())})
    groups = []
    for r in range(ZLINE):
        row = [blocks[r * place.rows_y]]
        for mask in place.x_bits:
            row = row + [swap(v, "expert", mask) for v in row]
        row = jnp.concatenate(row, axis=0)
        groups.append(jnp.concatenate([row, swap(row, "expert", 1)], axis=0))
    return groups


def scatter_tokens(place, groups, length):
    def add(left, right):
        return left.astype(f32) + right.astype(f32)

    reduced = []
    for part in groups:
        half = part.shape[0] // 2
        kept = add(part[:half], swap(part[half:], "expert", 1)).astype(bf16)
        for mask in place.x_bits[::-1]:
            half = kept.shape[0] // 2
            kept = add(kept[:half], swap(kept[half:], "expert", mask)).astype(bf16)
        reduced.append(kept)
    two = [add(reduced[i], swap(reduced[i + 2], "dp", place.z_bits[1])) for i in range(2)]
    return add(two[0], swap(two[1].astype(bf16), "dp", place.z_bits[0]))


def other(index, mask):
    return index + mask - 2 * mask * ((index // mask) % 2)


class Links:
    def __init__(self, sends, recvs):
        self.sends, self.recvs, self.used, self.open = sends, recvs, 0, []

    def copy(self, source, target, partner):
        at = self.used
        self.used += 1
        made = pltpu.make_async_remote_copy(
            src_ref=source,
            dst_ref=target,
            send_sem=self.sends.at[at],
            recv_sem=self.recvs.at[at],
            device_id=partner,
            device_id_type=pl.DeviceIdType.MESH,
        )
        made.start()
        self.open.append(made)
        return made

    def close(self):
        for made in self.open:
            made.wait_send()


def partners(rows_y):
    dp, ex = lax.axis_index("dp"), lax.axis_index("expert")
    return {
        "z1": (other(dp, rows_y), ex),
        "z2": (other(dp, 2 * rows_y), ex),
        "y": (other(dp, 1), ex),
        "x": (dp, other(ex, 2)),
        "c": (dp, other(ex, 1)),
    }


def greet(devices):
    barrier = pltpu.get_barrier_semaphore()
    for device in devices:
        pl.semaphore_signal(
            barrier, inc=1, device_id=device, device_id_type=pl.DeviceIdType.MESH
        )
    pl.semaphore_wait(barrier, len(devices))


MOE_COPIES = 22


def moe_kernel(
    rows_y,
    normed_ref,
    dy_hbm,
    gate_up_hbm,
    down_hbm,
    router_ref,
    spread_ref,
    rows_out,
    grads_out,
    acts_out,
    total_ref,
    w_gate,
    w_up,
    w_down,
    rows,
    dy,
    grads,
    acts,
    gate_grads,
    parts,
    heard_c,
    heard_x,
    heard_z2,
    heard_z1,
    sends,
    recvs,
    load_sems,
    dy_sems,
    out_sems,
):
    owned, hidden = w_down.shape[:2]
    length, width = normed_ref.shape
    count = rows.shape[1]
    half = count // 2
    span = owned * hidden
    z = lax.axis_index("dp") // rows_y
    to = partners(rows_y)
    links = Links(sends, recvs)

    loads = []
    mine = pl.ds(pl.multiple_of(z * hidden, hidden), hidden)
    theirs = pl.ds(pl.multiple_of(F + z * hidden, hidden), hidden)
    for e in range(owned):
        at = pl.ds(e * hidden, hidden)
        for k, (cut, kept) in enumerate(((mine, w_gate), (theirs, w_up))):
            loads.append(
                pltpu.make_async_copy(
                    gate_up_hbm.at[e, :, cut], kept.at[:, at], load_sems.at[2 * e + k]
                )
            )
    loads.append(pltpu.make_async_copy(down_hbm.at[:, mine, :], w_down, load_sems.at[2 * owned]))
    for load in loads:
        load.start()

    def fetch(r):
        return pltpu.make_async_copy(dy_hbm.at[r], dy.at[r % 2], dy_sems.at[r % 2])

    fetch(0).start()
    fetch(1).start()
    rows[0, :length] = normed_ref[...]
    greet([to["z1"], to["z2"], to["x"], to["c"]])

    own = pl.ds(0, length)
    pair = pl.ds(length, length)
    near, far = pl.ds(0, half), pl.ds(half, half)

    def row_x(r):
        return links.copy(rows.at[r, own], rows.at[r, pair], to["x"])

    def row_c(r):
        return links.copy(rows.at[r, near], rows.at[r, far], to["c"])

    z1 = links.copy(rows.at[0, own], rows.at[1, own], to["z1"])
    x0 = row_x(0)
    z2 = links.copy(rows.at[0, own], rows.at[2, own], to["z2"])
    x0.wait_recv()
    c0 = row_c(0)
    z1.wait_recv()
    x1 = row_x(1)
    z3 = links.copy(rows.at[1, own], rows.at[3, own], to["z2"])
    c0.wait_recv()
    for load in loads:
        load.wait()

    stores = []

    def store(source, target):
        made = pltpu.make_async_copy(source, target, out_sems.at[len(stores)])
        made.start()
        stores.append(made)
        return made

    def forward(r):
        slot = r % 2
        fetch(r).wait()
        logits = jnp.dot(rows[r], router_ref[...], preferred_element_type=f32)
        mask = dy[slot, :, width:].astype(f32) > 0.5
        logits = jnp.where(mask, logits, -1e30)
        lifted = jnp.where(
            mask, jnp.exp(logits - jnp.max(logits, axis=-1, keepdims=True)), 0.0
        )
        gates = lifted / jnp.sum(lifted, axis=-1, keepdims=True)
        gates_high = gates.astype(bf16)
        gates_low = (gates - gates_high.astype(f32)).astype(bf16)
        gate_grads[...] = jnp.zeros_like(gate_grads)

        def step(p, _):
            at = pl.ds(pl.multiple_of(p * 2 * hidden, 2 * hidden), 2 * hidden)
            up_at = pl.ds(pl.multiple_of(span + p * 2 * hidden, 2 * hidden), 2 * hidden)
            spread = spread_ref[:, at]
            down = w_down[pl.ds(2 * p, 2)].reshape(2 * hidden, width)
            gate_part = jnp.dot(rows[r], w_gate[:, at], preferred_element_type=f32)
            up_part = jnp.dot(rows[r], w_up[:, at], preferred_element_type=f32)
            plain_grad = against(dy[slot, :, :width], down)
            spread_gates = jnp.dot(gates_high, spread, preferred_element_type=f32) + jnp.dot(
                gates_low, spread, preferred_element_type=f32
            )
            sigmoid_gate = 1.0 / (1.0 + jnp.exp(-gate_part))
            swished = gate_part * sigmoid_gate
            activation = swished * up_part
            gate_grads[...] += against((plain_grad * activation).astype(bf16), spread)
            acts[slot, :, at] = (spread_gates * activation).astype(bf16)
            grad_act = plain_grad * spread_gates
            grads[r, :, at] = (
                grad_act * up_part * (sigmoid_gate + swished * (1.0 - sigmoid_gate))
            ).astype(bf16)
            grads[r, :, up_at] = (grad_act * swished).astype(bf16)
            return 0

        lax.fori_loop(0, owned // 2, step, 0)
        parts[r, :, width:] = gate_grads[...].astype(bf16)
        if r + 2 < ZLINE:
            fetch(r + 2).start()
        store(rows.at[r], rows_out.at[r])
        store(grads.at[r], grads_out.at[r])
        return store(acts.at[slot], acts_out.at[r])

    def backward(r):
        def step(j, _):
            at = pl.ds(pl.multiple_of(j * 512, 512), 512)
            part = against(grads[r, :, :span], w_gate[at, :]) + against(
                grads[r, :, span:], w_up[at, :]
            )
            parts[r, :, at] = part.astype(bf16)
            return 0

        lax.fori_loop(0, width // 512, step, 0)

    kept = [forward(0)]
    x1.wait_recv()
    c1 = row_c(1)
    z2.wait_recv()
    x2 = row_x(2)
    c1.wait_recv()
    kept.append(forward(1))
    x2.wait_recv()
    c2 = row_c(2)
    z3.wait_recv()
    x3 = row_x(3)
    c2.wait_recv()
    kept[0].wait()
    kept.append(forward(2))
    x3.wait_recv()
    c3 = row_c(3)
    c3.wait_recv()
    kept[1].wait()
    kept.append(forward(3))

    def add(left, right):
        return (left[...].astype(f32) + right[...].astype(f32)).astype(bf16)

    def part_c(r):
        return links.copy(parts.at[r, far], heard_c.at[r], to["c"])

    def part_x(r, copy):
        copy.wait_recv()
        parts[r, near] = add(parts.at[r, near], heard_c.at[r])
        return links.copy(parts.at[r, pair], heard_x.at[r], to["x"])

    def part_z(r, copy):
        copy.wait_recv()
        parts[r, own] = add(parts.at[r, own], heard_x.at[r])

    backward(3)
    c3 = part_c(3)
    backward(2)
    c2 = part_c(2)
    x3 = part_x(3, c3)
    backward(1)
    c1 = part_c(1)
    x2 = part_x(2, c2)
    part_z(3, x3)
    z3 = links.copy(parts.at[3, own], heard_z2.at[1], to["z2"])
    backward(0)
    c0 = part_c(0)
    x1 = part_x(1, c1)
    part_z(2, x2)
    z2 = links.copy(parts.at[2, own], heard_z2.at[0], to["z2"])
    x0 = part_x(0, c0)
    part_z(1, x1)
    z3.wait_recv()
    parts[1, own] = add(parts.at[1, own], heard_z2.at[1])
    z1 = links.copy(parts.at[1, own], heard_z1, to["z1"])
    part_z(0, x0)
    z2.wait_recv()
    total = parts[0, own].astype(f32) + heard_z2[0].astype(f32)
    z1.wait_recv()
    total_ref[...] = total + heard_z1[...].astype(f32)
    links.close()
    for k, made in enumerate(stores):
        if k not in (2, 5):
            made.wait()


def moe(rows_y, normed, dy, w_gate_up, w_down, router, spread):
    owned, width, _ = w_gate_up.shape
    hidden = F // ZLINE
    length = normed.shape[0]
    count = dy.shape[1]
    wide = width + 128
    any_space = pl.BlockSpec(memory_space=pl.ANY)
    vmem = pl.BlockSpec(memory_space=pltpu.VMEM)
    span = owned * hidden
    return pl.pallas_call(
        functools.partial(moe_kernel, rows_y),
        name="moe",
        out_shape=(
            jax.ShapeDtypeStruct((ZLINE, count, width), bf16),
            jax.ShapeDtypeStruct((ZLINE, count, 2 * span), bf16),
            jax.ShapeDtypeStruct((ZLINE, count, span), bf16),
            jax.ShapeDtypeStruct((length, wide), f32),
        ),
        in_specs=[vmem, any_space, any_space, any_space, vmem, vmem],
        out_specs=(any_space, any_space, any_space, vmem),
        scratch_shapes=[
            pltpu.VMEM((width, span), bf16),
            pltpu.VMEM((width, span), bf16),
            pltpu.VMEM((owned, hidden, width), bf16),
            pltpu.VMEM((ZLINE, count, width), bf16),
            pltpu.VMEM((2, count, wide), bf16),
            pltpu.VMEM((ZLINE, count, 2 * span), bf16),
            pltpu.VMEM((2, count, span), bf16),
            pltpu.VMEM((count, 128), f32),
            pltpu.VMEM((ZLINE, count, wide), bf16),
            pltpu.VMEM((ZLINE, count // 2, wide), bf16),
            pltpu.VMEM((ZLINE, length, wide), bf16),
            pltpu.VMEM((2, length, wide), bf16),
            pltpu.VMEM((length, wide), bf16),
            pltpu.SemaphoreType.DMA((MOE_COPIES,)),
            pltpu.SemaphoreType.DMA((MOE_COPIES,)),
            pltpu.SemaphoreType.DMA((2 * owned + 1,)),
            pltpu.SemaphoreType.DMA((2,)),
            pltpu.SemaphoreType.DMA((12,)),
        ],
        compiler_params=pltpu.CompilerParams(
            collective_id=1, has_side_effects=True, vmem_limit_bytes=60 * 2**20
        ),
    )(normed, dy, w_gate_up, w_down, router, spread)


def local(
    tokens,
    segments,
    routes,
    w_query,
    w_key,
    w_value,
    w_output,
    w_router,
    gain_attn,
    gain_moe,
    w_gate_up,
    w_down,
    cotangent,
):
    place = Place()
    length, width = tokens.shape
    owned = w_gate_up.shape[0]
    rows = w_query.shape[0]
    hidden = F // ZLINE
    per_group = H // KV
    q_end, k_end, v_end = H * HD, (H + KV) * HD, (H + 2 * KV) * HD
    o_end = v_end + width

    small = jnp.concatenate(
        [w_router, gain_attn[:, None], gain_moe[:, None], jnp.zeros((rows, 128 - EXPERTS - 2), bf16)],
        axis=1,
    )
    shard = jnp.concatenate([w_query, w_key, w_value, w_output, small], axis=1)
    full, order = gather_weights(place, shard)
    full_qkv, full_output = full[:, :v_end], full[:, v_end:o_end]
    full_small = transposed(order, full[:, o_end:]).astype(bf16)
    full_router = full_small[:, :EXPERTS]
    attn_gain = full_small[:, EXPERTS].astype(f32)
    moe_gain = full_small[:, EXPERTS + 1].astype(f32)

    chosen_mask = jnp.any(
        routes[:, :, None] == jnp.arange(EXPERTS, dtype=jnp.int32), axis=1
    )
    dy_block = jnp.concatenate(
        [cotangent, chosen_mask.astype(bf16), jnp.zeros((length, 128 - EXPERTS), bf16)], axis=1
    )
    dy_groups = gather_tokens(place, dy_block)

    cosine_table, sine_table = tables(length, HD)
    inputs = tokens.astype(f32)
    inv_attn = lax.rsqrt(jnp.mean(inputs * inputs, axis=-1, keepdims=True) + epsilon)
    unit_attn = inputs * inv_attn
    normed = (unit_attn * attn_gain).astype(bf16)
    normed = against(normed, order).astype(bf16)
    qkv = dot(normed, full_qkv)
    queries = rotate(qkv[:, :q_end].reshape(length, H, HD), cosine_table, sine_table)
    queries = queries.astype(bf16).reshape(length, KV, per_group, HD)
    key_rows = rotate(
        qkv[:, q_end:k_end].reshape(length, KV, HD), cosine_table, sine_table
    ).astype(bf16)
    values = qkv[:, k_end:].astype(bf16).reshape(length, KV, HD)
    segment = segments[0]
    position = jnp.arange(length, dtype=jnp.int32)
    allowed = (segment[:, None] == segment[None, :]) & (position[:, None] >= position[None, :])
    scores = (
        jnp.einsum("qkgd,skd->kgqs", queries, key_rows, preferred_element_type=f32) * 0.125
    )
    scores = jnp.where(allowed, scores, -1e30)
    maximum = jnp.max(scores, axis=-1, keepdims=True)
    lifted_scores = jnp.exp(scores - maximum)
    full_weights = lifted_scores / jnp.sum(lifted_scores, axis=-1, keepdims=True)
    attn_weights = full_weights.astype(bf16)
    mixed = jnp.einsum("kgqs,skd->qkgd", attn_weights, values, preferred_element_type=f32)
    mixed = mixed.reshape(length, H * HD).astype(bf16)
    mixed = against(mixed, order).astype(bf16)
    residual = inputs + dot(mixed, full_output)
    inv_moe = lax.rsqrt(jnp.mean(residual * residual, axis=-1, keepdims=True) + epsilon)
    unit_moe = residual * inv_moe
    normed_moe = (unit_moe * moe_gain).astype(bf16)

    def gates_of(rows_in, mask):
        logits = jnp.where(mask, dot(rows_in, full_router), -1e30)
        lifted = jnp.where(mask, jnp.exp(logits - jnp.max(logits, axis=-1, keepdims=True)), 0.0)
        return lifted / jnp.sum(lifted, axis=-1, keepdims=True)

    gates = gates_of(normed_moe, chosen_mask)

    def columns(start):
        cut = lax.dynamic_slice_in_dim(w_gate_up, start + place.z * hidden, hidden, 2)
        return cut.swapaxes(0, 1).reshape(width, owned * hidden)

    span = owned * hidden
    slice_down = lax.dynamic_slice_in_dim(w_down, place.z * hidden, hidden, 1)
    slice_down = slice_down.reshape(span, width)
    if place.ex_size == 4 and place.rows_y == 2:
        wide_router = jnp.pad(full_router, ((0, 0), (0, 128 - EXPERTS)))
        lane = jnp.arange(128, dtype=jnp.int32)[:, None]
        column = jnp.arange(span, dtype=jnp.int32)[None, :]
        spread = (lane == place.ex * owned + column // hidden).astype(bf16)
        all_dy = jnp.stack(dy_groups)
        all_rows, all_grads, all_acts, total = moe(
            place.rows_y, normed_moe, all_dy, w_gate_up, w_down, wide_router, spread
        )
        all_dy = all_dy[:, :, :width].reshape(-1, width)
        all_rows = all_rows.reshape(-1, width)
        all_grads = all_grads.reshape(-1, 2 * span)
        row_grads, grad_gates = total[:, :width], total[:, width : width + EXPERTS]
        out_parts = [dot(all_acts[r], slice_down).astype(bf16) for r in range(ZLINE)]
        all_acts = all_acts.reshape(-1, span)
    else:
        slice_gate_up = jnp.concatenate([columns(0), columns(F)], axis=1)
        moe_groups = gather_tokens(place, normed_moe)
        acts, grads_gate_up, gate_parts = [], [], []
        for normed_rows, dy_rows in zip(moe_groups, dy_groups):
            count = normed_rows.shape[0]
            group_gates = gates_of(normed_rows, dy_rows[:, width : width + EXPERTS] > 0.5)
            group_gates = lax.dynamic_slice_in_dim(group_gates, place.ex * owned, owned, 1)
            spread_gates = jnp.broadcast_to(group_gates[:, :, None], (count, owned, hidden))
            spread_gates = spread_gates.reshape(count, span)
            gate_up = dot(normed_rows, slice_gate_up)
            gate_part, up_part = gate_up[:, :span], gate_up[:, span:]
            plain_grad = against(dy_rows[:, :width], slice_down)
            sigmoid_gate = jax.nn.sigmoid(gate_part)
            swished = gate_part * sigmoid_gate
            activation = swished * up_part
            grad_act = plain_grad * spread_gates
            gate_parts.append(jnp.sum((plain_grad * activation).reshape(count, owned, hidden), axis=-1))
            acts.append((spread_gates * activation).astype(bf16))
            grads_gate_up.append(
                jnp.concatenate(
                    [
                        grad_act * up_part * sigmoid_gate * (1.0 + gate_part * (1.0 - sigmoid_gate)),
                        grad_act * swished,
                    ],
                    axis=-1,
                ).astype(bf16)
            )
        row_parts = [against(g, slice_gate_up).astype(bf16) for g in grads_gate_up]
        row_grads = scatter_tokens(place, row_parts, length)
        out_parts = [dot(a, slice_down).astype(bf16) for a in acts]
        gate_parts = [g.T for g in gate_parts]
        two = [gate_parts[i] + swap(gate_parts[i + 2], "dp", place.z_bits[1]) for i in range(2)]
        mine = two[0] + swap(two[1], "dp", place.z_bits[0])
        mine = mine.reshape(owned, 2, place.ex_size // 2, length)
        heard = [
            swap(mine[:, m % 2, m // 2], "expert", m) if m else mine[:, 0, 0]
            for m in range(place.ex_size)
        ]
        heard = jnp.stack(heard)
        grad_gates = jnp.concatenate(
            [pick(heard, place.ex ^ j) for j in range(place.ex_size)], axis=0
        ).T
        all_rows = jnp.concatenate([v for v in moe_groups], axis=0)
        all_dy = jnp.concatenate([v[:, :width] for v in dy_groups], axis=0)
        all_grads = jnp.concatenate(grads_gate_up, axis=0)
        all_acts = jnp.concatenate(acts, axis=0)
    output = (residual + scatter_tokens(place, out_parts, length)).astype(bf16)
    grad_logits = (
        gates * (grad_gates - jnp.sum(gates * grad_gates, axis=-1, keepdims=True))
    ).astype(bf16)

    def reduce_y(part, axis):
        part = jnp.moveaxis(part, axis, 0)
        for mask in place.y_bits[::-1]:
            at = (place.y // mask) % 2
            half = part.reshape((2, part.shape[0] // 2) + part.shape[1:])
            away = swap(pick(half, 1 - at), "dp", mask)
            part = (pick(half, at).astype(f32) + away.astype(f32)).astype(bf16)
        return part[0]

    shard_down = transposed(all_acts, all_dy).astype(bf16)
    shard_down = shard_down.reshape(owned, place.rows_y, hidden // place.rows_y, width)
    shard_down = reduce_y(shard_down, 1).astype(f32)
    part_gate_up = transposed(all_rows, all_grads).astype(bf16)
    part_gate_up = part_gate_up.reshape(ZLINE, place.rows_y, rows, 2 * span)
    part_gate_up = reduce_y(part_gate_up, 1)
    heard = [pick(part_gate_up, place.z)] + [
        swap(pick(part_gate_up, place.z ^ m), "dp", m * place.rows_y) for m in range(1, ZLINE)
    ]
    heard = jnp.stack(heard)
    shard_gate_up = jnp.stack([pick(heard, place.z ^ j) for j in range(ZLINE)], axis=0)
    shard_gate_up = shard_gate_up.reshape(ZLINE, rows, 2, owned, hidden)
    shard_gate_up = shard_gate_up.transpose(3, 1, 2, 0, 4).reshape(owned, rows, 2 * F).astype(f32)

    grad_out = cotangent.astype(f32)
    part_router = transposed(normed_moe, grad_logits)
    grad_normed_moe = row_grads + against(grad_logits, full_router)
    part_gain_moe = jnp.sum(grad_normed_moe * unit_moe, axis=0)
    scaled_moe = grad_normed_moe * moe_gain
    grad_residual = grad_out + inv_moe * (
        scaled_moe - unit_moe * jnp.mean(scaled_moe * unit_moe, axis=-1, keepdims=True)
    )
    grad_branch = grad_residual.astype(bf16)
    part_output = transposed(mixed, grad_branch)
    grad_mixed = dot(against(grad_branch, full_output).astype(bf16), order).astype(bf16)
    grad_mixed = grad_mixed.reshape(length, KV, per_group, HD)
    grad_weights = jnp.einsum(
        "qkgd,skd->kgqs", grad_mixed, values, preferred_element_type=f32
    )
    grad_values = jnp.einsum(
        "kgqs,qkgd->skd", attn_weights, grad_mixed, preferred_element_type=f32
    )
    grad_values = grad_values.astype(bf16).reshape(length, KV * HD)
    grad_scores = (
        full_weights * (grad_weights - jnp.sum(full_weights * grad_weights, axis=-1, keepdims=True))
    ).astype(bf16)
    grad_queries = (
        jnp.einsum("kgqs,skd->qkgd", grad_scores, key_rows, preferred_element_type=f32) * 0.125
    )
    grad_queries = rotate(grad_queries.reshape(length, H, HD), cosine_table, -sine_table)
    grad_queries = grad_queries.astype(bf16).reshape(length, H * HD)
    grad_keys = (
        jnp.einsum("kgqs,qkgd->skd", grad_scores, queries, preferred_element_type=f32) * 0.125
    )
    grad_keys = rotate(grad_keys, cosine_table, -sine_table)
    grad_keys = grad_keys.astype(bf16).reshape(length, KV * HD)
    grad_qkv = jnp.concatenate([grad_queries, grad_keys, grad_values], axis=1)
    part_qkv = transposed(normed, grad_qkv)
    grad_normed = against(grad_qkv, full_qkv)
    grad_normed = lax.dot_general(
        grad_normed,
        order.astype(f32),
        (((1,), (0,)), ((), ())),
        precision=lax.Precision.HIGHEST,
        preferred_element_type=f32,
    )
    part_gain_attn = jnp.sum(grad_normed * unit_attn, axis=0)
    scaled_attn = grad_normed * attn_gain
    grad_tokens = (
        grad_residual
        + inv_attn
        * (scaled_attn - unit_attn * jnp.mean(scaled_attn * unit_attn, axis=-1, keepdims=True))
    ).astype(bf16)
    part_small = jnp.concatenate(
        [
            part_router.astype(bf16),
            part_gain_attn[:, None].astype(bf16),
            part_gain_moe[:, None].astype(bf16),
            jnp.zeros((width, 128 - EXPERTS - 2), bf16),
        ],
        axis=1,
    )
    part_small = dot(order, part_small).astype(bf16)
    summed = scatter_weights(
        place,
        jnp.concatenate([part_qkv.astype(bf16), part_output.astype(bf16), part_small], axis=1),
    )
    return (
        output,
        grad_tokens,
        summed[:, :q_end],
        summed[:, q_end:k_end],
        summed[:, k_end:v_end],
        summed[:, v_end:o_end],
        summed[:, o_end : o_end + EXPERTS],
        summed[:, o_end + EXPERTS],
        summed[:, o_end + EXPERTS + 1],
        shard_gate_up,
        shard_down,
    )


def solution(mesh):
    return jax.shard_map(
        local,
        mesh=mesh,
        in_specs=(
            P(("dp", "expert"), None),
            P(("dp", "expert"), None),
            P(("dp", "expert"), None),
            P("dp", None),
            P("dp", None),
            P("dp", None),
            P("dp", None),
            P("dp", None),
            P("dp"),
            P("dp"),
            P("expert", None, None),
            P("expert", None, None),
            P(("dp", "expert"), None),
        ),
        out_specs=(
            P(("dp", "expert"), None),
            P(("dp", "expert"), None),
            P("dp", None),
            P("dp", None),
            P("dp", None),
            P("dp", None),
            P("dp", None),
            P("dp"),
            P("dp"),
            P("expert", "dp", None),
            P("expert", "dp", None),
        ),
        check_vma=False,
    )
```

time: 1800 us -> 820 us (0.46)
  waiting for transfers between devices: 1430 us -> 414 us
  Pallas kernels: 0 us -> 120 us
  blocking collectives: 85.4 us -> 0 us
  matrix products: 123 us -> 83.4 us
  starting transfers between devices: 21.1 us -> 57.3 us
  local copies, waits for them, and re-layouts: 51.4 us -> 76.2 us
    reduce_scatter x6 -> x0, waiting for transfers between devices: 1050 us -> none  [the longest x1 494 us: local(): lax.psum_scatter(part_gate_up.astype(jnp.bfloat16), 'dp', scatter_dimensi...]
    ppermute x0 -> x60, waiting for transfers between devices: none -> 414 us  [swap(): return lax.ppermute(value, axis, [(i, i ^ mask) for i in range(size)])]
    all_gather x4 -> x0, waiting for transfers between devices: 201 us -> none  [the longest x1 78.7 us: local(): lax.all_gather(w_query, 'dp', axis=0, tiled=True)]
    all_to_all x4 -> x0, waiting for transfers between devices: 129 us -> none  [the longest x1 44.6 us: local(): lax.all_to_all(grad_rows, 'expert', split_axis=0, concat_axis=0, tiled=True)]
    pallas_call x0 -> x1, Pallas kernels: none -> 120 us  [moe(): pl.pallas_call(functools.partial(moe_kernel, rows_y), name='moe', out_sha...]
    dot_general x14 -> x12, matrix products: 98.6 us -> 29.9 us  [the longest x9 23.7 us: dot(): return jnp.dot(left_side, right_side, preferred_element_type=f32)]
    ppermute x0 -> x60, starting transfers between devices: none -> 57.3 us  [swap(): return lax.ppermute(value, axis, [(i, i ^ mask) for i in range(size)])]
    unnamed x2 -> x0, blocking collectives: 44.2 us -> none
  transfers between devices with their start and end apart: 16 -> 60, of which waited for: 16 -> 29; matrix products, arithmetic and copies ran while one was open for 8% -> 17% of each run, Pallas kernels for 0% -> 0%
where the time goes in v1:
time: 820 us; the launch traced here: 805 us
  waiting for transfers between devices  414 us (50%)
  Pallas kernels  120 us (15%)
  matrix products  83.4 us (10%)
  local copies, waits for them, and re-layouts  76.2 us (9%)
  starting transfers between devices  57.3 us (7%)
  other arithmetic  51.2 us (6%)
    ppermute x60, waiting for transfers between devices, swap(): return lax.ppermute(value, axis, [(i, i ^ mask) for i in range(size)])  414 us
    pallas_call x1, Pallas kernels, moe(): pl.pallas_call(functools.partial(moe_kernel, rows_y), name='moe', out_sha...  120 us
    ppermute x60, starting transfers between devices, swap(): return lax.ppermute(value, axis, [(i, i ^ mask) for i in range(size)])  57.3 us
    dot_general x6, matrix products, transposed(): lax.dot_general(left_side, right_side, (((0,), (0,)), ((), ())), preferre...  43.1 us
    convert_element_type x3, local copies, waits for them, and re-layouts, local(): shard_gate_up.transpose(3, 1, 2, 0, 4).reshape(owned, rows, 2 * F)  31.8 us
    dot_general x9, matrix products, dot(): return jnp.dot(left_side, right_side, preferred_element_type=f32)  23.7 us
  transfers between devices with their start and end apart: 60, of which 29 were waited for; matrix products, arithmetic and copies ran while one was open for 17% of the time, Pallas kernels for 0%

profile of v1, /device:TPU:0, one launch (start us, length us, event | category | flops | bytes accessed | tf_op | source)
XLA Modules:
  0.0 805.1 jit_solution(8273746489741845001)
XLA Ops:
  28.0 26.5 %collective-permute-done.23 = bf16[128,1664]{1,0:T(8,128)(2,1)S(1)} collective-permute-done((bf16[128,1664]{1,0:T(8,128)(2,1)S(1)}, bf16[128,1664]{1,0:T(8,128)(2,1)S(1)}, u32[]{:S(2)}, u32[]{:S(2)}) %collective-permute-start.23) | collective-permute-done | bytes 426016 | tf_op jit(solution)/shard_map/ppermute | solution.py:61
  62.5 21.1 %collective-permute-done.1 = bf16[32,4224]{1,0:T(8,128)(2,1)S(1)} collective-permute-done((bf16[32,4224]{1,0:T(8,128)(2,1)S(1)}, bf16[32,4224]{1,0:T(8,128)(2,1)S(1)}, u32[]{:S(2)}, u32[]{:S(2)}) %collective-permute-start.1) | collective-permute-done | bytes 270368 | tf_op jit(solution)/shard_map/ppermute | solution.py:61
  103.6 9.6 %collective-permute-done.6 = bf16[2,32,4224]{2,1,0:T(8,128)(2,1)S(1)} collective-permute-done((bf16[2,32,4224]{2,1,0:T(8,128)(2,1)}, bf16[2,32,4224]{2,1,0:T(8,128)(2,1)S(1)}, u32[]{:S(2)}, u32[]{:S(2)}) %collective-permute-start.6) | collective-permute-done | bytes 540704 | tf_op jit(solution)/shard_map/ppermute | solution.py:61
  113.3 7.9 collective-permute-done.12
  126.6 8.2 %collective-permute-done.30 = bf16[128,1664]{1,0:T(8,128)(2,1)S(1)} collective-permute-done((bf16[128,1664]{1,0:T(8,128)(2,1)S(1)}, bf16[128,1664]{1,0:T(8,128)(2,1)S(1)}, u32[]{:S(2)}, u32[]{:S(2)}) %collective-permute-start.30) | collective-permute-done | bytes 426016 | tf_op jit(solution)/shard_map/ppermute | solution.py:61
  136.6 7.3 collective-permute-done.7
  159.8 11.5 %collective-permute-done.18 = bf16[2,32,4224]{2,1,0:T(8,128)(2,1)S(1)} collective-permute-done((bf16[2,32,4224]{2,1,0:T(8,128)(2,1)S(1)}, bf16[2,32,4224]{2,1,0:T(8,128)(2,1)S(1)}, u32[]{:S(2)}, u32[]{:S(2)}) %collective-permute-start.18) | collective-permute-done | bytes 540704 | tf_op jit(solution)/shard_map/ppermute | solution.py:61
  205.8 120.1 %moe.1 = (bf16[4,512,1536]{2,1,0:T(8,128)(2,1)}, bf16[4,512,2560]{2,1,0:T(8,128)(2,1)}, bf16[4,512,1280]{2,1,0:T(8,128)(2,1)}, f32[128,1664]{1,0:T(8,128)}) custom-call(bf16[128,1536]{1,0:T(8,128)(2,1)} %multiply_convert_fusion.normed_ref, bf16[4,512,1664]{2,1,0:T(8,128)(2,1)} %pad_maximum_fusion.1.dy_hbm, bf16[10,1536,1024]{2,1,0:T(8,128)(2,1)} %gate_up_hbm.1, ...), custom_call_target="tpu_custom_call" | custom-call | tf_op jit(solution)/shard_map/moe/pallas_call | solution.py:461
  356.9 20.4 %collective-permute-done.40 = bf16[128,1536]{1,0:T(8,128)(2,1)S(1)} collective-permute-done((bf16[128,1536]{1,0:T(8,128)(2,1)S(1)}, bf16[128,1536]{1,0:T(8,128)(2,1)S(1)}, u32[]{:S(2)}, u32[]{:S(2)}) %collective-permute-start.40) | collective-permute-done | bytes 393248 | tf_op jit(solution)/shard_map/ppermute | solution.py:61
  384.8 19.8 %collective-permute-done.41 = bf16[128,1536]{1,0:T(8,128)(2,1)S(1)} collective-permute-done((bf16[128,1536]{1,0:T(8,128)(2,1)S(1)}, bf16[128,1536]{1,0:T(8,128)(2,1)S(1)}, u32[]{:S(2)}, u32[]{:S(2)}) %collective-permute-start.41) | collective-permute-done | bytes 393248 | tf_op jit(solution)/shard_map/ppermute | solution.py:61
  413.0 8.3 %collective-permute-done.42 = bf16[128,1536]{1,0:T(8,128)(2,1)S(1)} collective-permute-done((bf16[128,1536]{1,0:T(8,128)(2,1)S(1)}, bf16[128,1536]{1,0:T(8,128)(2,1)S(1)}, u32[]{:S(2)}, u32[]{:S(2)}) %collective-permute-start.42) | collective-permute-done | bytes 393248 | tf_op jit(solution)/shard_map/ppermute | solution.py:61
  454.5 12.1 %fusion.9 = bf16[1280,1536]{1,0:T(8,128)(2,1)S(1)} fusion(bf16[4,512,1280]{2,1,0:T(8,128)(2,1)} %get-tuple-element.15, bf16[4,512,1664]{2,1,0:T(8,128)(2,1)} %pad_maximum_fusion.1.dy_hbm), kind=kOutput, calls=%fused_computation.17 | convolution fusion | flops 8055029760 | bytes 15466496 | tf_op jit(solution)/shard_map/dot_general | solution.py:48
  468.6 21.1 %bitcast_convert_fusion = bf16[1536,2560]{1,0:T(8,128)(2,1)S(1)} fusion(bf16[4,512,1536]{2,1,0:T(8,128)(2,1)} %get-tuple-element.17, bf16[4,512,2560]{2,1,0:T(8,128)(2,1)} %get-tuple-element.18), kind=kOutput, calls=%fused_computation.1 | convolution fusion | flops 16110059520 | bytes 24641536 | tf_op jit(solution)/shard_map/dot_general | solution.py:48
  494.8 8.9 %fusion.1 = bf16[8,3,32,4224]{3,2,1,0:T(8,128)(2,1)} fusion(bf16[8,3,32,4224]{3,2,1,0:T(8,128)(2,1)} %collective-permute-done.43, bf16[8,3,2,32,4224]{4,3,2,1,0:T(8,128)(2,1)} %bitcast.298), kind=kLoop, calls=%fused_computation.4 | loop fusion | flops 12976128 | bytes 19464192 | tf_op jit(solution)/shard_map/convert_element_type | solution.py:133
  518.5 36.3 %collective-permute-done.44 = bf16[8,32,4224]{2,1,0:T(8,128)(2,1)S(1)} collective-permute-done((bf16[8,32,4224]{2,1,0:T(8,128)(2,1)S(1)}, bf16[8,32,4224]{2,1,0:T(8,128)(2,1)S(1)}, u32[]{:S(2)}, u32[]{:S(2)}) %collective-permute-start.44) | collective-permute-done | bytes 2162720 | tf_op jit(solution)/shard_map/ppermute | solution.py:61
  560.1 71.4 %collective-permute-done.49 = bf16[2,32,4224]{2,1,0:T(8,128)(2,1)S(1)} collective-permute-done((bf16[2,32,4224]{2,1,0:T(8,128)(2,1)S(1)}, bf16[2,32,4224]{2,1,0:T(8,128)(2,1)S(1)}, u32[]{:S(2)}, u32[]{:S(2)}) %collective-permute-start.49) | collective-permute-done | bytes 540704 | tf_op jit(solution)/shard_map/ppermute | solution.py:61
  634.8 7.9 collective-permute-done.48
  642.7 25.7 %collective-permute-done.50 = bf16[2,32,4224]{2,1,0:T(8,128)(2,1)S(1)} collective-permute-done((bf16[2,32,4224]{2,1,0:T(8,128)(2,1)S(1)}, bf16[2,32,4224]{2,1,0:T(8,128)(2,1)S(1)}, u32[]{:S(2)}, u32[]{:S(2)}) %collective-permute-start.50) | collective-permute-done | bytes 540704 | tf_op jit(solution)/shard_map/ppermute | solution.py:61
  680.1 32.6 %collective-permute-done.51 = bf16[2,32,4224]{2,1,0:T(8,128)(2,1)S(1)} collective-permute-done((bf16[2,32,4224]{2,1,0:T(8,128)(2,1)S(1)}, bf16[2,32,4224]{2,1,0:T(8,128)(2,1)S(1)}, u32[]{:S(2)}, u32[]{:S(2)}) %collective-permute-start.51) | collective-permute-done | bytes 540704 | tf_op jit(solution)/shard_map/ppermute | solution.py:61
  714.4 40.3 %collective-permute-done.56 = bf16[192,2560]{1,0:T(8,128)(2,1)S(1)} collective-permute-done((bf16[192,2560]{1,0:T(8,128)(2,1)S(1)}, bf16[192,2560]{1,0:T(8,128)(2,1)S(1)}, u32[]{:S(2)}, u32[]{:S(2)}) %collective-permute-start.56) | collective-permute-done | bytes 983072 | tf_op jit(solution)/shard_map/ppermute | solution.py:61
  756.7 7.0 collective-permute-done.53
  767.7 10.3 %copy.253 = f32[4,192,2560]{1,2,0:T(8,128)} copy(f32[4,192,2560]{2,1,0:T(8,128)} %maximum_convert_fusion) | data formatting | bytes 15728640 | tf_op jit(solution)/shard_map/convert_element_type | solution.py:676
  778.0 11.4 %copy.254 = f32[10,192,2,4,128]{4,3,2,1,0:T(4,128)} copy(f32[10,192,2,4,128]{1,4,0,2,3:T(8,128)} %bitcast.299) | data formatting | bytes 15728640 | tf_op jit(solution)/shard_map/convert_element_type | solution.py:676
  789.5 10.1 %reshape.410 = f32[10,192,1024]{2,1,0:T(8,128)} reshape(f32[10,192,2,4,128]{4,3,2,1,0:T(4,128)} %copy.254) | data formatting | bytes 15728640 | tf_op jit(solution)/shard_map/convert_element_type | solution.py:676
  (425 shorter events, 246.3 us)
Async XLA Ops:
  7.9 46.6 %collective-permute-start = (bf16[2,32,4224]{2,1,0:T(8,128)(2,1)}, bf16[2,32,4224]{2,1,0:T(8,128)(2,1)}, u32[]{:S(2)}, u32[]{:S(2)}) collective-permute-start(bf16[2,32,4224]{2,1,0:T(8,128)(2,1)} %pad_maximum_fusion.17), channel_id=1, source_target_pairs={{0,4},{4,0},{8,12},{12,8},{16,20},{20,16},{24,28},{28,24},{1,5},{5... | collective-permute-start | bytes 1622024 | tf_op jit(solution)/shard_map/ppermute | solution.py:61
  10.8 47.6 %collective-permute-start.3 = (bf16[2,32,4224]{2,1,0:T(8,128)(2,1)}, bf16[2,32,4224]{2,1,0:T(8,128)(2,1)}, u32[]{:S(2)}, u32[]{:S(2)}) collective-permute-start(bf16[2,32,4224]{2,1,0:T(8,128)(2,1)} %pad_maximum_fusion.17), channel_id=1, source_target_pairs={{0,8},{4,12},{8,0},{12,4},{16,24},{20,28},{24,16},{28,20},{1,9},{5... | collective-permute-start | bytes 1622024 | tf_op jit(solution)/shard_map/ppermute | solution.py:61
  12.4 47.5 %collective-permute-start.9 = (bf16[2,32,4224]{2,1,0:T(8,128)(2,1)}, bf16[2,32,4224]{2,1,0:T(8,128)(2,1)}, u32[]{:S(2)}, u32[]{:S(2)}) collective-permute-start(bf16[2,32,4224]{2,1,0:T(8,128)(2,1)} %pad_maximum_fusion.17), channel_id=1, source_target_pairs={{0,16},{4,20},{8,24},{12,28},{16,0},{20,4},{24,8},{28,12},{1,17},{... | collective-permute-start | bytes 1622024 | tf_op jit(solution)/shard_map/ppermute | solution.py:61
  54.5 80.4 %collective-permute-start.22 = (bf16[256,1664]{1,0:T(8,128)(2,1)S(1)}, bf16[256,1664]{1,0:T(8,128)(2,1)S(1)}, u32[]{:S(2)}, u32[]{:S(2)}) collective-permute-start(bf16[256,1664]{1,0:T(8,128)(2,1)S(1)} %pad_maximum_fusion.4), channel_id=1, source_target_pairs={{0,1},{1,0},{2,3},{3,2},{4,5},{5,4},{6,7},{7,6},{8,9},{9,8},{10,11... | collective-permute-start | bytes 2555912 | tf_op jit(solution)/shard_map/ppermute | solution.py:61
  54.5 66.7 %collective-permute-start.29 = (bf16[128,1664]{1,0:T(8,128)(2,1)S(1)}, bf16[128,1664]{1,0:T(8,128)(2,1)S(1)}, u32[]{:S(2)}, u32[]{:S(2)}) collective-permute-start(bf16[128,1664]{1,0:T(8,128)(2,1)S(1)} %collective-permute-done.23), channel_id=1, source_target_pairs={{0,16},{4,20},{8,24},{12,28},{16,0},{20,4},{24,8},{28,12},{1,17},{... | collective-permute-start | bytes 1277960 | tf_op jit(solution)/shard_map/ppermute | solution.py:61
  56.9 42.8 %collective-permute-start.24 = (bf16[128,1664]{1,0:T(8,128)(2,1)S(1)}, bf16[128,1664]{1,0:T(8,128)(2,1)S(1)}, u32[]{:S(2)}, u32[]{:S(2)}) collective-permute-start(bf16[128,1664]{1,0:T(8,128)(2,1)S(1)} %collective-permute-done.23), channel_id=1, source_target_pairs={{0,2},{1,3},{2,0},{3,1},{4,6},{5,7},{6,4},{7,5},{8,10},{9,11},{10,... | collective-permute-start | bytes 1277960 | tf_op jit(solution)/shard_map/ppermute | solution.py:61
  58.4 42.9 %collective-permute-start.27 = (bf16[128,1664]{1,0:T(8,128)(2,1)S(1)}, bf16[128,1664]{1,0:T(8,128)(2,1)S(1)}, u32[]{:S(2)}, u32[]{:S(2)}) collective-permute-start(bf16[128,1664]{1,0:T(8,128)(2,1)S(1)} %collective-permute-done.26), channel_id=1, source_target_pairs={{0,2},{1,3},{2,0},{3,1},{4,6},{5,7},{6,4},{7,5},{8,10},{9,11},{10,... | collective-permute-start | bytes 1277960 | tf_op jit(solution)/shard_map/ppermute | solution.py:61
  113.3 58.1 %collective-permute-start.2 = (bf16[3,32,4224]{2,1,0:T(8,128)(2,1)S(1)}, bf16[3,32,4224]{2,1,0:T(8,128)(2,1)S(1)}, u32[]{:S(2)}, u32[]{:S(2)}) collective-permute-start(bf16[3,32,4224]{2,1,0:T(8,128)(2,1)S(1)} %get-tuple-element.146), channel_id=1, source_target_pairs={{0,1},{1,0},{2,3},{3,2},{4,5},{5,4},{6,7},{7,6},{8,9},{9,8},{10,11... | collective-permute-start | bytes 2433032 | tf_op jit(solution)/shard_map/ppermute | solution.py:61
  121.2 51.0 %collective-permute-start.5 = (bf16[3,32,4224]{2,1,0:T(8,128)(2,1)S(1)}, bf16[3,32,4224]{2,1,0:T(8,128)(2,1)S(1)}, u32[]{:S(2)}, u32[]{:S(2)}) collective-permute-start(bf16[3,32,4224]{2,1,0:T(8,128)(2,1)S(1)} %get-tuple-element.144), channel_id=1, source_target_pairs={{0,1},{1,0},{2,3},{3,2},{4,5},{5,4},{6,7},{7,6},{8,9},{9,8},{10,11... | collective-permute-start | bytes 2433032 | tf_op jit(solution)/shard_map/ppermute | solution.py:61
  121.2 65.7 %collective-permute-start.11 = (bf16[3,32,4224]{2,1,0:T(8,128)(2,1)S(1)}, bf16[3,32,4224]{2,1,0:T(8,128)(2,1)S(1)}, u32[]{:S(2)}, u32[]{:S(2)}) collective-permute-start(bf16[3,32,4224]{2,1,0:T(8,128)(2,1)S(1)} %get-tuple-element.140), channel_id=1, source_target_pairs={{0,1},{1,0},{2,3},{3,2},{4,5},{5,4},{6,7},{7,6},{8,9},{9,8},{10,11... | collective-permute-start | bytes 2433032 | tf_op jit(solution)/shard_map/ppermute | solution.py:61
  348.4 58.4 %collective-permute-start.33 = (bf16[128,1536]{1,0:T(8,128)(2,1)S(1)}, bf16[128,1536]{1,0:T(8,128)(2,1)S(1)}, u32[]{:S(2)}, u32[]{:S(2)}) collective-permute-start(bf16[128,1536]{1,0:T(8,128)(2,1)S(1)} %slice.350), channel_id=1, source_target_pairs={{0,2},{1,3},{2,0},{3,1},{4,6},{5,7},{6,4},{7,5},{8,10},{9,11},{10,... | collective-permute-start | bytes 1179656 | tf_op jit(solution)/shard_map/ppermute | solution.py:61
  466.8 45.8 %collective-permute-start.59 = (bf16[1,10,64,1536]{3,2,1,0:T(8,128)(2,1)S(1)}, bf16[1,10,64,1536]{3,2,1,0:T(8,128)(2,1)}, u32[]{:S(2)}, u32[]{:S(2)}) collective-permute-start(bf16[1,10,64,1536]{3,2,1,0:T(8,128)(2,1)S(1)} %dynamic-slice_bitcast_fusion.1), channel_id=1, source_target_pairs={{0,4},{4,0},{8,12},{12,8},{16,20},{20,16},{24,28},{28,24},{1,5},{5... | collective-permute-start | bytes 5898248 | tf_op jit(solution)/shard_map/ppermute | solution.py:61
  494.1 174.6 %collective-permute-start.55 = (bf16[1,4,192,2560]{3,2,1,0:T(8,128)(2,1)}, bf16[1,4,192,2560]{3,2,1,0:T(8,128)(2,1)}, u32[]{:S(2)}, u32[]{:S(2)}) collective-permute-start(bf16[1,4,192,2560]{3,2,1,0:T(8,128)(2,1)} %dynamic-slice_bitcast_fusion), channel_id=1, source_target_pairs={{0,4},{4,0},{8,12},{12,8},{16,20},{20,16},{24,28},{28,24},{1,5},{5... | collective-permute-start | bytes 11796488 | tf_op jit(solution)/shard_map/ppermute | solution.py:61
  505.6 49.2 %collective-permute-start.44 = (bf16[8,32,4224]{2,1,0:T(8,128)(2,1)S(1)}, bf16[8,32,4224]{2,1,0:T(8,128)(2,1)S(1)}, u32[]{:S(2)}, u32[]{:S(2)}) collective-permute-start(bf16[8,32,4224]{2,1,0:T(8,128)(2,1)S(1)} %slice_bitcast_fusion.2), channel_id=1, source_target_pairs={{0,2},{1,3},{2,0},{3,1},{4,6},{5,7},{6,4},{7,5},{8,10},{9,11},{10,... | collective-permute-start | bytes 6488072 | tf_op jit(solution)/shard_map/ppermute | solution.py:61
  555.6 119.4 %collective-permute-start.45 = (bf16[2,32,4224]{2,1,0:T(8,128)(2,1)S(1)}, bf16[2,32,4224]{2,1,0:T(8,128)(2,1)S(1)}, u32[]{:S(2)}, u32[]{:S(2)}) collective-permute-start(bf16[2,32,4224]{2,1,0:T(8,128)(2,1)S(1)} %pad_maximum_fusion.18), channel_id=1, source_target_pairs={{0,4},{4,0},{8,12},{12,8},{16,20},{20,16},{24,28},{28,24},{1,5},{5... | collective-permute-start | bytes 1622024 | tf_op jit(solution)/shard_map/ppermute | solution.py:61
  557.1 74.6 %collective-permute-start.46 = (bf16[2,32,4224]{2,1,0:T(8,128)(2,1)S(1)}, bf16[2,32,4224]{2,1,0:T(8,128)(2,1)S(1)}, u32[]{:S(2)}, u32[]{:S(2)}) collective-permute-start(bf16[2,32,4224]{2,1,0:T(8,128)(2,1)S(1)} %pad_maximum_fusion.19), channel_id=1, source_target_pairs={{0,4},{4,0},{8,12},{12,8},{16,20},{20,16},{24,28},{28,24},{1,5},{5... | collective-permute-start | bytes 1622024 | tf_op jit(solution)/shard_map/ppermute | solution.py:61
  557.9 73.6 %collective-permute-start.49 = (bf16[2,32,4224]{2,1,0:T(8,128)(2,1)S(1)}, bf16[2,32,4224]{2,1,0:T(8,128)(2,1)S(1)}, u32[]{:S(2)}, u32[]{:S(2)}) collective-permute-start(bf16[2,32,4224]{2,1,0:T(8,128)(2,1)S(1)} %pad_maximum_fusion.21), channel_id=1, source_target_pairs={{0,4},{4,0},{8,12},{12,8},{16,20},{20,16},{24,28},{28,24},{1,5},{5... | collective-permute-start | bytes 1622024 | tf_op jit(solution)/shard_map/ppermute | solution.py:61
  559.4 83.3 %collective-permute-start.48 = (bf16[2,32,4224]{2,1,0:T(8,128)(2,1)S(1)}, bf16[2,32,4224]{2,1,0:T(8,128)(2,1)S(1)}, u32[]{:S(2)}, u32[]{:S(2)}) collective-permute-start(bf16[2,32,4224]{2,1,0:T(8,128)(2,1)S(1)} %pad_maximum_fusion.20), channel_id=1, source_target_pairs={{0,4},{4,0},{8,12},{12,8},{16,20},{20,16},{24,28},{28,24},{1,5},{5... | collective-permute-start | bytes 1622024 | tf_op jit(solution)/shard_map/ppermute | solution.py:61
  631.9 48.2 %collective-permute-start.47 = (bf16[2,32,4224]{2,1,0:T(8,128)(2,1)S(1)}, bf16[2,32,4224]{2,1,0:T(8,128)(2,1)S(1)}, u32[]{:S(2)}, u32[]{:S(2)}) collective-permute-start(bf16[2,32,4224]{2,1,0:T(8,128)(2,1)S(1)} %add_convert_fusion.9), channel_id=1, source_target_pairs={{0,16},{4,20},{8,24},{12,28},{16,0},{20,4},{24,8},{28,12},{1,17},{... | collective-permute-start | bytes 1622024 | tf_op jit(solution)/shard_map/ppermute | solution.py:61
  668.6 44.0 %collective-permute-start.51 = (bf16[2,32,4224]{2,1,0:T(8,128)(2,1)S(1)}, bf16[2,32,4224]{2,1,0:T(8,128)(2,1)S(1)}, u32[]{:S(2)}, u32[]{:S(2)}) collective-permute-start(bf16[2,32,4224]{2,1,0:T(8,128)(2,1)S(1)} %add_convert_fusion.5), channel_id=1, source_target_pairs={{0,8},{4,12},{8,0},{12,4},{16,24},{20,28},{24,16},{28,20},{1,9},{5... | collective-permute-start | bytes 1622024 | tf_op jit(solution)/shard_map/ppermute | solution.py:61
  672.1 82.5 %collective-permute-start.56 = (bf16[192,2560]{1,0:T(8,128)(2,1)S(1)}, bf16[192,2560]{1,0:T(8,128)(2,1)S(1)}, u32[]{:S(2)}, u32[]{:S(2)}) collective-permute-start(bf16[192,2560]{1,0:T(8,128)(2,1)S(1)} %get-tuple-element.108), channel_id=1, source_target_pairs={{0,8},{4,12},{8,0},{12,4},{16,24},{20,28},{24,16},{28,20},{1,9},{5... | collective-permute-start | bytes 2949128 | tf_op jit(solution)/shard_map/ppermute | solution.py:61
  674.2 80.5 %collective-permute-start.57 = (bf16[192,2560]{1,0:T(8,128)(2,1)S(1)}, bf16[192,2560]{1,0:T(8,128)(2,1)S(1)}, u32[]{:S(2)}, u32[]{:S(2)}) collective-permute-start(bf16[192,2560]{1,0:T(8,128)(2,1)S(1)} %get-tuple-element.107), channel_id=1, source_target_pairs={{0,16},{4,20},{8,24},{12,28},{16,0},{20,4},{24,8},{28,12},{1,17},{... | collective-permute-start | bytes 2949128 | tf_op jit(solution)/shard_map/ppermute | solution.py:61
  675.0 79.7 %collective-permute-start.58 = (bf16[192,2560]{1,0:T(8,128)(2,1)S(1)}, bf16[192,2560]{1,0:T(8,128)(2,1)S(1)}, u32[]{:S(2)}, u32[]{:S(2)}) collective-permute-start(bf16[192,2560]{1,0:T(8,128)(2,1)S(1)} %get-tuple-element.106), channel_id=1, source_target_pairs={{0,24},{4,28},{8,16},{12,20},{16,8},{20,12},{24,0},{28,4},{1,25},{... | collective-permute-start | bytes 2949128 | tf_op jit(solution)/shard_map/ppermute | solution.py:61
  713.0 43.6 %collective-permute-start.52 = (bf16[32,4224]{1,0:T(8,128)(2,1)S(1)}, bf16[32,4224]{1,0:T(8,128)(2,1)S(1)}, u32[]{:S(2)}, u32[]{:S(2)}) collective-permute-start(bf16[32,4224]{1,0:T(8,128)(2,1)S(1)} %get-tuple-element.151), channel_id=1, source_target_pairs={{0,2},{1,3},{2,0},{3,1},{4,6},{5,7},{6,4},{7,5},{8,10},{9,11},{10,... | collective-permute-start | bytes 811016 | tf_op jit(solution)/shard_map/ppermute | solution.py:61
  (116 other events, 2483.8 us)

commit v2 on v1

--- a/solution.py
+++ b/solution.py
@@ -229,6 +229,199 @@
             barrier, inc=1, device_id=device, device_id_type=pl.DeviceIdType.MESH
         )
     pl.semaphore_wait(barrier, len(devices))
+
+
+def gather_kernel(rows_y, exclusive, *refs):
+    shards, dy = refs[:3], refs[3]
+    fulls, dy_all = refs[4:7], refs[7]
+    z_send, z_recv, y_send, y_recv, x_send, x_recv, c_send, c_recv = refs[8:16]
+    dz_send, dz_recv, dx_send, dx_recv, dc_send, dc_recv, local_sems = refs[16:]
+    n = shards[0].shape[0]
+    half = n // 2
+    piece = half - exclusive
+    length = dy.shape[0]
+    dp, ex = lax.axis_index("dp"), lax.axis_index("expert")
+    z, y = dp // rows_y, dp % rows_y
+    core, side = ex % 2, (ex // 2) % 2
+    to = partners(rows_y)
+    z_of = [z, other(z, 1), other(z, 2), other(other(z, 1), 2)]
+
+    in_plane = pl.ds(pl.multiple_of(core * half + side * exclusive, 16), piece)
+    alone = pl.ds(pl.multiple_of(core * half + side * piece, 16), exclusive)
+    of_core = pl.ds(pl.multiple_of(core * half, 16), half)
+
+    def remote(source, target, send_sem, recv_sem, device):
+        return pltpu.make_async_remote_copy(
+            src_ref=source,
+            dst_ref=target,
+            send_sem=send_sem,
+            recv_sem=recv_sem,
+            device_id=device,
+            device_id_type=pl.DeviceIdType.MESH,
+        )
+
+    def copies(rows, m, ys, send, recv, at, device, own=False):
+        made = []
+        for k in range(3):
+            block = fulls[k].at[z_of[m] * rows_y + ys, rows]
+            source = shards[k].at[rows] if own else block
+            made.append(remote(source, block, send.at[k, at], recv.at[k, at], device))
+        return made
+
+    def to_z(step):
+        m, device = ((0, "z1"), (0, "z2"), (2, "z1"))[step]
+        return copies(in_plane, m, y, z_send, z_recv, step, to[device], m == 0)
+
+    def to_y(m):
+        return copies(in_plane, m, y, y_send, y_recv, m, to["y"], m == 0)
+
+    def to_x(m, k):
+        ys = 1 - y if k else y
+        return copies(alone, m, ys, x_send, x_recv, 2 * m + k, to["x"])
+
+    def to_c(m, k):
+        ys = 1 - y if k else y
+        return copies(of_core, m, ys, c_send, c_recv, 2 * m + k, to["c"])
+
+    near, pair = pl.ds(0, length), pl.ds(length, length)
+    front, back = pl.ds(0, 2 * length), pl.ds(2 * length, 2 * length)
+
+    def dy_z(step):
+        m, target, device = ((0, 1, "z1"), (0, 2, "z2"), (2, 3, "z1"))[step]
+        source = dy_all.at[m, near] if m else dy
+        return remote(
+            source, dy_all.at[target, near], dz_send.at[step], dz_recv.at[step], to[device]
+        )
+
+    def dy_x(m):
+        source = dy_all.at[m, near] if m else dy
+        return remote(source, dy_all.at[m, pair], dx_send.at[m], dx_recv.at[m], to["x"])
+
+    def dy_c(m):
+        return remote(
+            dy_all.at[m, front], dy_all.at[m, back], dc_send.at[m], dc_recv.at[m], to["c"]
+        )
+
+    mine = [
+        pltpu.make_async_copy(shards[k], fulls[k].at[dp], local_sems.at[k]) for k in range(3)
+    ]
+    mine.append(pltpu.make_async_copy(dy, dy_all.at[0, near], local_sems.at[3]))
+    for made in mine:
+        made.start()
+    greet([to["z1"], to["z2"], to["y"], to["x"], to["c"]])
+
+    def start(made):
+        for copy in made:
+            copy.start()
+
+    def arrived(made):
+        for copy in made:
+            copy.wait_recv()
+
+    start(to_z(1))
+    start(to_z(0))
+    start(to_y(0))
+    dy_x(0).start()
+    dy_z(1).start()
+    dy_z(0).start()
+
+    arrived(to_z(0))
+    start(to_y(1))
+    start(to_x(1, 0))
+    arrived(to_z(1))
+    start(to_z(2))
+    start(to_y(2))
+    start(to_x(2, 0))
+    dy_z(0).wait_recv()
+    dy_x(1).start()
+    dy_z(1).wait_recv()
+    dy_z(2).start()
+    dy_x(2).start()
+    arrived(to_y(0))
+    start(to_x(0, 1))
+    dy_x(0).wait_recv()
+    mine[3].wait()
+    dy_c(0).start()
+    arrived(to_z(2))
+    start(to_y(3))
+    start(to_x(3, 0))
+    arrived(to_y(1))
+    start(to_x(1, 1))
+    dy_x(1).wait_recv()
+    dy_c(1).start()
+    dy_z(2).wait_recv()
+    dy_x(3).start()
+    for m in (1, 2):
+        arrived(to_x(m, 0))
+        start(to_c(m, 0))
+    arrived(to_x(0, 1))
+    start(to_c(0, 1))
+    arrived(to_y(2))
+    start(to_x(2, 1))
+    dy_x(2).wait_recv()
+    dy_c(2).start()
+    arrived(to_x(1, 1))
+    start(to_c(1, 1))
+    arrived(to_y(3))
+    start(to_x(3, 1))
+    for m, k in ((3, 0), (2, 1), (3, 1)):
+        arrived(to_x(m, k))
+        start(to_c(m, k))
+    dy_x(3).wait_recv()
+    dy_c(3).start()
+
+    for made in mine[:3]:
+        made.wait()
+    for step in range(3):
+        for made in to_z(step):
+            made.wait_send()
+        dy_z(step).wait_send()
+    for m in range(ZLINE):
+        for made in to_y(m):
+            made.wait_send()
+        dy_x(m).wait_send()
+        dy_c(m).wait()
+        for k in range(2):
+            if m or k:
+                for made in to_x(m, k):
+                    made.wait_send()
+                for made in to_c(m, k):
+                    made.wait()
+
+
+def gather(rows_y, shards, dy):
+    exclusive = shards[0].shape[0] // 12
+    dp_size = ZLINE * rows_y
+    any_space = pl.BlockSpec(memory_space=pl.ANY)
+    sems = pltpu.SemaphoreType.DMA
+    return pl.pallas_call(
+        functools.partial(gather_kernel, rows_y, exclusive),
+        name="gather",
+        out_shape=tuple(jax.ShapeDtypeStruct((dp_size,) + v.shape, bf16) for v in shards)
+        + (jax.ShapeDtypeStruct((ZLINE, 4 * dy.shape[0], dy.shape[1]), bf16),),
+        in_specs=[pl.BlockSpec(memory_space=pltpu.VMEM)] * 4,
+        out_specs=(any_space,) * 4,
+        scratch_shapes=[
+            sems((3, 3)),
+            sems((3, 3)),
+            sems((3, ZLINE)),
+            sems((3, ZLINE)),
+            sems((3, dp_size)),
+            sems((3, dp_size)),
+            sems((3, dp_size)),
+            sems((3, dp_size)),
+            sems((3,)),
+            sems((3,)),
+            sems((ZLINE,)),
+            sems((ZLINE,)),
+            sems((ZLINE,)),
+            sems((ZLINE,)),
+            sems((4,)),
+        ],
+        compiler_params=pltpu.CompilerParams(
+            collective_id=2, has_side_effects=True, vmem_limit_bytes=60 * 2**20
+        ),
+    )(*shards, dy)
 
 
 MOE_COPIES = 22
@@ -495,6 +688,431 @@
     )(normed, dy, w_gate_up, w_down, router, spread)
 
 
+def finish_kernel(
+    rows_y,
+    rows_hbm,
+    grads_hbm,
+    acts_hbm,
+    dy_hbm,
+    att_hbm,
+    gate_up_out,
+    down_out,
+    att_out,
+    wide,
+    turned,
+    grads,
+    acts,
+    part_gate_up,
+    heard_gate_up,
+    heard_z,
+    part_down,
+    heard_down,
+    stage_gate_up,
+    stage_down,
+    own,
+    heard_c,
+    heard_x,
+    heard_z1,
+    heard_z2,
+    heard_y,
+    load_sems,
+    grads_sems,
+    acts_sems,
+    store_sems,
+    down_store_sems,
+    y_send,
+    y_recv,
+    d_send,
+    d_recv,
+    z_send,
+    z_recv,
+    a_send,
+    a_recv,
+):
+    owned, n = gate_up_out.shape[:2]
+    hidden = F // ZLINE
+    count, width = wide.shape[1:]
+    tokens = ZLINE * count
+    columns = att_out.shape[1]
+    dp, ex = lax.axis_index("dp"), lax.axis_index("expert")
+    z, y = dp // rows_y, dp % rows_y
+    core, side = ex % 2, (ex // 2) % 2
+    to = partners(rows_y)
+    to["z3"] = (other(to["z1"][0], 2 * rows_y), ex)
+    z_of = [z, other(z, 1), other(z, 2), other(other(z, 1), 2)]
+    half, quarter = n // 2, n // 4
+    of_core = pl.ds(pl.multiple_of(core * half, 16), half)
+    of_sibling = pl.ds(pl.multiple_of((1 - core) * half, 16), half)
+    of_side = pl.ds(pl.multiple_of(side * quarter, 16), quarter)
+    of_far_side = pl.ds(pl.multiple_of((1 - side) * quarter, 16), quarter)
+
+    def remote(source, target, send_sem, recv_sem, device):
+        return pltpu.make_async_remote_copy(
+            src_ref=source,
+            dst_ref=target,
+            send_sem=send_sem,
+            recv_sem=recv_sem,
+            device_id=device,
+            device_id_type=pl.DeviceIdType.MESH,
+        )
+
+    def add(left, right):
+        return (left.astype(f32) + right.astype(f32)).astype(bf16)
+
+    def load_wide(source, r):
+        return pltpu.make_async_copy(source.at[r, :, pl.ds(0, width)], wide.at[r], load_sems.at[r])
+
+    load_own = pltpu.make_async_copy(att_hbm.at[:, of_core], own, load_sems.at[ZLINE])
+
+    def load_acts(e):
+        at = pl.ds(pl.multiple_of(e * hidden, hidden), hidden)
+        return pltpu.make_async_copy(
+            acts_hbm.at[:, :, at], acts.at[lax.rem(e, 2)], acts_sems.at[lax.rem(e, 2)]
+        )
+
+    def load_grads(e, k):
+        at = pl.ds(pl.multiple_of((k * owned + e) * hidden, hidden), hidden)
+        return pltpu.make_async_copy(
+            grads_hbm.at[:, :, at],
+            grads.at[lax.rem(e, 2), :, :, pl.ds(k * hidden, hidden)],
+            grads_sems.at[lax.rem(e, 2), k],
+        )
+
+    load_acts(0).start()
+    for r in range(ZLINE):
+        load_wide(dy_hbm, r).start()
+    load_acts(1).start()
+    load_own.start()
+    for e in range(2):
+        for k in range(2):
+            load_grads(e, k).start()
+    greet([to["z1"], to["z2"], to["z3"], to["y"], to["x"], to["c"]])
+
+    cuts = [pl.ds(0, 2048), pl.ds(2048, columns - 2048)]
+
+    def att(k, step, source, target, device):
+        return remote(source, target, a_send.at[k, step], a_recv.at[k, step], device)
+
+    def att_c(k):
+        return att(
+            k, 0, att_hbm.at[:, of_sibling, cuts[k]], heard_c.at[:, :, cuts[k]], to["c"]
+        )
+
+    def att_x(k):
+        return att(
+            k, 1, own.at[:, of_far_side, cuts[k]], heard_x.at[:, :, cuts[k]], to["x"]
+        )
+
+    def line(m):
+        return pl.ds(z_of[m] * rows_y, rows_y)
+
+    def att_z1(k, m):
+        return att(
+            k, 2 + m, own.at[line(1 + 2 * m), of_side, cuts[k]], heard_z1.at[m, :, :, cuts[k]], to["z1"]
+        )
+
+    def att_z2(k):
+        return att(k, 4, own.at[line(2), of_side, cuts[k]], heard_z2.at[:, :, cuts[k]], to["z2"])
+
+    def att_y(k):
+        return att(
+            k, 5, own.at[other(dp, 1), of_side, cuts[k]], heard_y.at[:, cuts[k]], to["y"]
+        )
+
+    mine = pl.ds(pl.multiple_of(core * half + side * quarter, 16), quarter)
+
+    def att_back_x(k):
+        return att(k, 6, att_out.at[mine, cuts[k]], att_out.at[mine, cuts[k]], to["x"])
+
+    def att_back_c(k):
+        return att(k, 7, att_out.at[of_core, cuts[k]], att_out.at[of_core, cuts[k]], to["c"])
+
+    def att_after_c(k):
+        att_c(k).wait_recv()
+
+        def step(b, _):
+            own[b, :, cuts[k]] = add(own[b, :, cuts[k]], heard_c[b, :, cuts[k]])
+            return 0
+
+        lax.fori_loop(0, own.shape[0], step, 0)
+        att_x(k).start()
+
+    def att_after_x(k):
+        att_x(k).wait_recv()
+
+        def step(b, _):
+            own[b, of_side, cuts[k]] = add(own[b, of_side, cuts[k]], heard_x[b, :, cuts[k]])
+            return 0
+
+        lax.fori_loop(0, own.shape[0], step, 0)
+        for m in range(2):
+            att_z1(k, m).start()
+
+    def att_after_z1(k):
+        for m in (1, 0):
+            att_z1(k, m).wait_recv()
+            own[line(2 * m), of_side, cuts[k]] = add(
+                own[line(2 * m), of_side, cuts[k]], heard_z1[m, :, :, cuts[k]]
+            )
+            if m:
+                att_z2(k).start()
+
+    def att_after_z2(k):
+        att_z2(k).wait_recv()
+        own[line(0), of_side, cuts[k]] = add(
+            own[line(0), of_side, cuts[k]], heard_z2[:, :, cuts[k]]
+        )
+        att_y(k).start()
+
+    def att_after_y(k):
+        att_y(k).wait_recv()
+        att_out[mine, cuts[k]] = add(own[dp, of_side, cuts[k]], heard_y[:, cuts[k]])
+        att_back_x(k).start()
+
+    def att_after_back(k):
+        att_back_x(k).wait_recv()
+        att_back_c(k).start()
+
+    for k in range(2):
+        att_c(k).start()
+
+    def send_down(e):
+        return remote(
+            part_down.at[e, 1 - y], heard_down.at[e], d_send.at[e], d_recv.at[e], to["y"]
+        )
+
+    for r in range(ZLINE):
+        load_wide(dy_hbm, r).wait()
+
+    early = 3
+
+    def down(e, _):
+        load_acts(e).wait()
+        left = acts[lax.rem(e, 2)].reshape(tokens, hidden)
+
+        def step(j, _):
+            at = pl.ds(pl.multiple_of(j * 512, 512), 512)
+            result = transposed(left, wide[:, :, at].reshape(tokens, 512)).astype(bf16)
+            for k in range(rows_y):
+                part_down[e, k, :, at] = result[k * (hidden // rows_y) : (k + 1) * (hidden // rows_y)]
+            return 0
+
+        lax.fori_loop(0, width // 512, step, 0)
+
+        @pl.when(e + 2 < owned)
+        def _():
+            load_acts(e + 2).start()
+
+        @pl.when(e < early)
+        def _():
+            send_down(e).start()
+
+        return 0
+
+    lax.fori_loop(0, owned, down, 0)
+    for r in range(ZLINE):
+        load_wide(rows_hbm, r).start()
+    load_own.wait()
+    att_after_c(0)
+    for r in range(ZLINE):
+        load_wide(rows_hbm, r).wait()
+
+        def turn(j, _, r=r):
+            at = pl.ds(pl.multiple_of(j * 256, 256), 256)
+            turned[at, pl.ds(r * count, count)] = wide[r, :, at].T
+            return 0
+
+        lax.fori_loop(0, width // 256, turn, 0)
+
+    def send_y(e):
+        return remote(
+            part_gate_up.at[e, 1 - y], heard_gate_up.at[e], y_send.at[e], y_recv.at[e], to["y"]
+        )
+
+    def send_z(e, m):
+        return remote(
+            part_gate_up.at[e, y, z_of[m]],
+            heard_z.at[m - 1, e],
+            z_send.at[m - 1, e],
+            z_recv.at[m - 1, e],
+            to[f"z{m}"],
+        )
+
+    def reduce(e):
+        send_y(e).wait_recv()
+        for b in range(ZLINE):
+            part_gate_up[e, y, b] = add(part_gate_up[e, y, b], heard_gate_up[e, b])
+        for m in range(1, ZLINE):
+            send_z(e, m).start()
+
+    def gate_up(e, _):
+        for k in range(2):
+            load_grads(e, k).wait()
+        right = grads[lax.rem(e, 2)].reshape(tokens, 2 * hidden)
+
+        def step(b, _):
+            at = pl.ds(pl.multiple_of(b * rows_y * n, 128), rows_y * n)
+            result = jnp.dot(turned[at, :], right, preferred_element_type=f32).astype(bf16)
+            for k in range(rows_y):
+                part_gate_up[e, k, b] = result[k * n : (k + 1) * n]
+            return 0
+
+        lax.fori_loop(0, ZLINE, step, 0)
+
+        @pl.when(e + 2 < owned)
+        def _():
+            for k in range(2):
+                load_grads(e + 2, k).start()
+
+        send_y(e).start()
+
+        @pl.when(e >= 2)
+        def _():
+            reduce(e - 2)
+
+        return 0
+
+    lax.fori_loop(0, 1, gate_up, 0)
+    att_after_c(1)
+    lax.fori_loop(1, 5, gate_up, 0)
+    att_after_x(0)
+    lax.fori_loop(5, 8, gate_up, 0)
+    att_after_z1(0)
+    lax.fori_loop(8, owned, gate_up, 0)
+    att_after_x(1)
+    for e in range(early, early + 2):
+        send_down(e).start()
+    reduce(owned - 2)
+    reduce(owned - 1)
+    for e in range(early + 2, owned):
+        send_down(e).start()
+    att_after_z2(0)
+
+    def keep_gate_up(e):
+        return pltpu.make_async_copy(
+            stage_gate_up.at[lax.rem(e, 2)], gate_up_out.at[e], store_sems.at[lax.rem(e, 2)]
+        )
+
+    def finish_gate_up(e, _):
+        slot = lax.rem(e, 2)
+
+        @pl.when(e >= 2)
+        def _():
+            keep_gate_up(e - 2).wait()
+
+        for m in range(ZLINE):
+            if m:
+                send_z(e, m).wait_recv()
+                block = heard_z[m - 1, e]
+            else:
+                block = part_gate_up[e, y, z]
+            for k in range(2):
+                at = pl.ds(pl.multiple_of(k * F + z_of[m] * hidden, hidden), hidden)
+                stage_gate_up[slot, :, at] = block[:, k * hidden : (k + 1) * hidden].astype(f32)
+        keep_gate_up(e).start()
+        return 0
+
+    def keep_down(e):
+        return pltpu.make_async_copy(
+            stage_down.at[lax.rem(e, 2)], down_out.at[e], down_store_sems.at[lax.rem(e, 2)]
+        )
+
+    def finish_down(e, _):
+        @pl.when(e >= 2)
+        def _():
+            keep_down(e - 2).wait()
+
+        send_down(e).wait_recv()
+        stage_down[lax.rem(e, 2)] = part_down[e, y].astype(f32) + heard_down[e].astype(f32)
+        keep_down(e).start()
+        return 0
+
+    att_after_z1(1)
+    lax.fori_loop(0, owned - 2, finish_gate_up, 0)
+    att_after_y(0)
+    att_after_z2(1)
+    lax.fori_loop(0, owned - 3, finish_down, 0)
+    att_after_back(0)
+    lax.fori_loop(owned - 2, owned, finish_gate_up, 0)
+    att_after_y(1)
+    lax.fori_loop(owned - 3, owned, finish_down, 0)
+    att_after_back(1)
+
+    for e in (owned - 2, owned - 1):
+        keep_gate_up(e).wait()
+        keep_down(e).wait()
+
+    def close(e, _):
+        send_y(e).wait_send()
+        send_down(e).wait_send()
+        for m in range(1, ZLINE):
+            send_z(e, m).wait_send()
+        return 0
+
+    lax.fori_loop(0, owned, close, 0)
+    for k in range(2):
+        att_back_c(k).wait()
+        for made in (att_c(k), att_x(k), att_z1(k, 0), att_z1(k, 1), att_z2(k), att_y(k)):
+            made.wait_send()
+        att_back_x(k).wait_send()
+
+
+def finish(rows_y, rows, grads, acts, dy, att):
+    _, count, width = rows.shape
+    span = acts.shape[2]
+    hidden = F // ZLINE
+    owned = span // hidden
+    dp_size, n, columns = att.shape
+    any_space = pl.BlockSpec(memory_space=pl.ANY)
+    sems = pltpu.SemaphoreType.DMA
+    return pl.pallas_call(
+        functools.partial(finish_kernel, rows_y),
+        name="finish",
+        out_shape=(
+            jax.ShapeDtypeStruct((owned, n, 2 * F), f32),
+            jax.ShapeDtypeStruct((owned, hidden // rows_y, width), f32),
+            jax.ShapeDtypeStruct((n, columns), bf16),
+        ),
+        in_specs=[any_space] * 5,
+        out_specs=(any_space, any_space, pl.BlockSpec(memory_space=pltpu.VMEM)),
+        scratch_shapes=[
+            pltpu.VMEM((ZLINE, count, width), bf16),
+            pltpu.VMEM((width, ZLINE * count), bf16),
+            pltpu.VMEM((2, ZLINE, count, 2 * hidden), bf16),
+            pltpu.VMEM((2, ZLINE, count, hidden), bf16),
+            pltpu.VMEM((owned, rows_y, ZLINE, n, 2 * hidden), bf16),
+            pltpu.VMEM((owned, ZLINE, n, 2 * hidden), bf16),
+            pltpu.VMEM((ZLINE - 1, owned, n, 2 * hidden), bf16),
+            pltpu.VMEM((owned, rows_y, hidden // rows_y, width), bf16),
+            pltpu.VMEM((owned, hidden // rows_y, width), bf16),
+            pltpu.VMEM((2, n, 2 * F), f32),
+            pltpu.VMEM((2, hidden // rows_y, width), f32),
+            pltpu.VMEM((dp_size, n // 2, columns), bf16),
+            pltpu.VMEM((dp_size, n // 2, columns), bf16),
+            pltpu.VMEM((dp_size, n // 4, columns), bf16),
+            pltpu.VMEM((2, rows_y, n // 4, columns), bf16),
+            pltpu.VMEM((rows_y, n // 4, columns), bf16),
+            pltpu.VMEM((n // 4, columns), bf16),
+            sems((ZLINE + 1,)),
+            sems((2, 2)),
+            sems((2,)),
+            sems((2,)),
+            sems((2,)),
+            sems((owned,)),
+            sems((owned,)),
+            sems((owned,)),
+            sems((owned,)),
+            sems((ZLINE - 1, owned)),
+            sems((ZLINE - 1, owned)),
+            sems((2, 8)),
+            sems((2, 8)),
+        ],
+        compiler_params=pltpu.CompilerParams(
+            collective_id=3, has_side_effects=True, vmem_limit_bytes=63 * 2**20
+        ),
+    )(rows, grads, acts, dy, att)
+
+
 def local(
     tokens,
     segments,
@@ -523,28 +1141,55 @@
         [w_router, gain_attn[:, None], gain_moe[:, None], jnp.zeros((rows, 128 - EXPERTS - 2), bf16)],
         axis=1,
     )
-    shard = jnp.concatenate([w_query, w_key, w_value, w_output, small], axis=1)
-    full, order = gather_weights(place, shard)
-    full_qkv, full_output = full[:, :v_end], full[:, v_end:o_end]
-    full_small = transposed(order, full[:, o_end:]).astype(bf16)
-    full_router = full_small[:, :EXPERTS]
-    attn_gain = full_small[:, EXPERTS].astype(f32)
-    moe_gain = full_small[:, EXPERTS + 1].astype(f32)
-
     chosen_mask = jnp.any(
         routes[:, :, None] == jnp.arange(EXPERTS, dtype=jnp.int32), axis=1
     )
     dy_block = jnp.concatenate(
         [cotangent, chosen_mask.astype(bf16), jnp.zeros((length, 128 - EXPERTS), bf16)], axis=1
     )
-    dy_groups = gather_tokens(place, dy_block)
+    kernels = place.ex_size == 4 and place.rows_y == 2
+    if kernels:
+        qkv_shard = jnp.concatenate([w_query, w_key, w_value], axis=1)
+        full_qkv, full_output, full_small, all_dy = gather(
+            place.rows_y, (qkv_shard, w_output, small), dy_block
+        )
+        full_qkv = full_qkv.reshape(width, v_end)
+        full_output = full_output.reshape(width, width)
+        full_small = full_small.reshape(width, 128)
+
+        def ordered(value):
+            return value
+
+        canonical = ordered
+    else:
+        shard = jnp.concatenate([w_query, w_key, w_value, w_output, small], axis=1)
+        full, order = gather_weights(place, shard)
+        full_qkv, full_output = full[:, :v_end], full[:, v_end:o_end]
+        full_small = transposed(order, full[:, o_end:]).astype(bf16)
+        dy_groups = gather_tokens(place, dy_block)
+
+        def ordered(value):
+            return against(value, order).astype(bf16)
+
+        def canonical(value):
+            return lax.dot_general(
+                value,
+                order.astype(value.dtype),
+                (((1,), (0,)), ((), ())),
+                precision=lax.Precision.HIGHEST,
+                preferred_element_type=f32,
+            ).astype(value.dtype)
+
+    full_router = full_small[:, :EXPERTS]
+    attn_gain = full_small[:, EXPERTS].astype(f32)
+    moe_gain = full_small[:, EXPERTS + 1].astype(f32)
 
     cosine_table, sine_table = tables(length, HD)
     inputs = tokens.astype(f32)
     inv_attn = lax.rsqrt(jnp.mean(inputs * inputs, axis=-1, keepdims=True) + epsilon)
     unit_attn = inputs * inv_attn
     normed = (unit_attn * attn_gain).astype(bf16)
-    normed = against(normed, order).astype(bf16)
+    normed = ordered(normed)
     qkv = dot(normed, full_qkv)
     queries = rotate(qkv[:, :q_end].reshape(length, H, HD), cosine_table, sine_table)
     queries = queries.astype(bf16).reshape(length, KV, per_group, HD)
@@ -565,7 +1210,7 @@
     attn_weights = full_weights.astype(bf16)
     mixed = jnp.einsum("kgqs,skd->qkgd", attn_weights, values, preferred_element_type=f32)
     mixed = mixed.reshape(length, H * HD).astype(bf16)
-    mixed = against(mixed, order).astype(bf16)
+    mixed = ordered(mixed)
     residual = inputs + dot(mixed, full_output)
     inv_moe = lax.rsqrt(jnp.mean(residual * residual, axis=-1, keepdims=True) + epsilon)
     unit_moe = residual * inv_moe
@@ -585,21 +1230,16 @@
     span = owned * hidden
     slice_down = lax.dynamic_slice_in_dim(w_down, place.z * hidden, hidden, 1)
     slice_down = slice_down.reshape(span, width)
-    if place.ex_size == 4 and place.rows_y == 2:
+    if kernels:
         wide_router = jnp.pad(full_router, ((0, 0), (0, 128 - EXPERTS)))
         lane = jnp.arange(128, dtype=jnp.int32)[:, None]
         column = jnp.arange(span, dtype=jnp.int32)[None, :]
         spread = (lane == place.ex * owned + column // hidden).astype(bf16)
-        all_dy = jnp.stack(dy_groups)
         all_rows, all_grads, all_acts, total = moe(
             place.rows_y, normed_moe, all_dy, w_gate_up, w_down, wide_router, spread
         )
-        all_dy = all_dy[:, :, :width].reshape(-1, width)
-        all_rows = all_rows.reshape(-1, width)
-        all_grads = all_grads.reshape(-1, 2 * span)
         row_grads, grad_gates = total[:, :width], total[:, width : width + EXPERTS]
         out_parts = [dot(all_acts[r], slice_down).astype(bf16) for r in range(ZLINE)]
-        all_acts = all_acts.reshape(-1, span)
     else:
         slice_gate_up = jnp.concatenate([columns(0), columns(F)], axis=1)
         moe_groups = gather_tokens(place, normed_moe)
@@ -652,29 +1292,6 @@
         gates * (grad_gates - jnp.sum(gates * grad_gates, axis=-1, keepdims=True))
     ).astype(bf16)
 
-    def reduce_y(part, axis):
-        part = jnp.moveaxis(part, axis, 0)
-        for mask in place.y_bits[::-1]:
-            at = (place.y // mask) % 2
-            half = part.reshape((2, part.shape[0] // 2) + part.shape[1:])
-            away = swap(pick(half, 1 - at), "dp", mask)
-            part = (pick(half, at).astype(f32) + away.astype(f32)).astype(bf16)
-        return part[0]
-
-    shard_down = transposed(all_acts, all_dy).astype(bf16)
-    shard_down = shard_down.reshape(owned, place.rows_y, hidden // place.rows_y, width)
-    shard_down = reduce_y(shard_down, 1).astype(f32)
-    part_gate_up = transposed(all_rows, all_grads).astype(bf16)
-    part_gate_up = part_gate_up.reshape(ZLINE, place.rows_y, rows, 2 * span)
-    part_gate_up = reduce_y(part_gate_up, 1)
-    heard = [pick(part_gate_up, place.z)] + [
-        swap(pick(part_gate_up, place.z ^ m), "dp", m * place.rows_y) for m in range(1, ZLINE)
-    ]
-    heard = jnp.stack(heard)
-    shard_gate_up = jnp.stack([pick(heard, place.z ^ j) for j in range(ZLINE)], axis=0)
-    shard_gate_up = shard_gate_up.reshape(ZLINE, rows, 2, owned, hidden)
-    shard_gate_up = shard_gate_up.transpose(3, 1, 2, 0, 4).reshape(owned, rows, 2 * F).astype(f32)
-
     grad_out = cotangent.astype(f32)
     part_router = transposed(normed_moe, grad_logits)
     grad_normed_moe = row_grads + against(grad_logits, full_router)
@@ -685,7 +1302,7 @@
     )
     grad_branch = grad_residual.astype(bf16)
     part_output = transposed(mixed, grad_branch)
-    grad_mixed = dot(against(grad_branch, full_output).astype(bf16), order).astype(bf16)
+    grad_mixed = canonical(against(grad_branch, full_output).astype(bf16))
     grad_mixed = grad_mixed.reshape(length, KV, per_group, HD)
     grad_weights = jnp.einsum(
         "qkgd,skd->kgqs", grad_mixed, values, preferred_element_type=f32
@@ -709,14 +1326,7 @@
     grad_keys = grad_keys.astype(bf16).reshape(length, KV * HD)
     grad_qkv = jnp.concatenate([grad_queries, grad_keys, grad_values], axis=1)
     part_qkv = transposed(normed, grad_qkv)
-    grad_normed = against(grad_qkv, full_qkv)
-    grad_normed = lax.dot_general(
-        grad_normed,
-        order.astype(f32),
-        (((1,), (0,)), ((), ())),
-        precision=lax.Precision.HIGHEST,
-        preferred_element_type=f32,
-    )
+    grad_normed = canonical(against(grad_qkv, full_qkv))
     part_gain_attn = jnp.sum(grad_normed * unit_attn, axis=0)
     scaled_attn = grad_normed * attn_gain
     grad_tokens = (
@@ -733,11 +1343,45 @@
         ],
         axis=1,
     )
-    part_small = dot(order, part_small).astype(bf16)
-    summed = scatter_weights(
-        place,
-        jnp.concatenate([part_qkv.astype(bf16), part_output.astype(bf16), part_small], axis=1),
-    )
+    if kernels:
+        parts = jnp.concatenate([part_qkv.astype(bf16), part_output.astype(bf16), part_small], axis=1)
+        shard_gate_up, shard_down, summed = finish(
+            place.rows_y,
+            all_rows,
+            all_grads,
+            all_acts,
+            all_dy,
+            parts.reshape(place.dp_size, rows, -1),
+        )
+        summed = summed.astype(f32)
+    else:
+        part_small = dot(order, part_small).astype(bf16)
+        summed = scatter_weights(
+            place,
+            jnp.concatenate([part_qkv.astype(bf16), part_output.astype(bf16), part_small], axis=1),
+        )
+        def reduce_y(part, axis):
+            part = jnp.moveaxis(part, axis, 0)
+            for mask in place.y_bits[::-1]:
+                at = (place.y // mask) % 2
+                half = part.reshape((2, part.shape[0] // 2) + part.shape[1:])
+                away = swap(pick(half, 1 - at), "dp", mask)
+                part = (pick(half, at).astype(f32) + away.astype(f32)).astype(bf16)
+            return part[0]
+
+        shard_down = transposed(all_acts, all_dy).astype(bf16)
+        shard_down = shard_down.reshape(owned, place.rows_y, hidden // place.rows_y, width)
+        shard_down = reduce_y(shard_down, 1).astype(f32)
+        part_gate_up = transposed(all_rows, all_grads).astype(bf16)
+        part_gate_up = part_gate_up.reshape(ZLINE, place.rows_y, rows, 2 * span)
+        part_gate_up = reduce_y(part_gate_up, 1)
+        heard = [pick(part_gate_up, place.z)] + [
+            swap(pick(part_gate_up, place.z ^ m), "dp", m * place.rows_y) for m in range(1, ZLINE)
+        ]
+        heard = jnp.stack(heard)
+        shard_gate_up = jnp.stack([pick(heard, place.z ^ j) for j in range(ZLINE)], axis=0)
+        shard_gate_up = shard_gate_up.reshape(ZLINE, rows, 2, owned, hidden)
+        shard_gate_up = shard_gate_up.transpose(3, 1, 2, 0, 4).reshape(owned, rows, 2 * F).astype(f32)
     return (
         output,
         grad_tokens,

time: 820 us -> 579 us (0.71); the launches traced: 805 us -> 572 us
  waiting for transfers between devices: 414 us -> 35.3 us
  Pallas kernels: 120 us -> 397 us
  starting transfers between devices: 57.3 us -> 7.17 us
  matrix products: 83.4 us -> 45.8 us
  other arithmetic: 51.2 us -> 23.9 us
  local copies, waits for them, and re-layouts: 76.2 us -> 61.9 us
    ppermute x60 -> x11, waiting for transfers between devices: 414 us -> 35.3 us  [swap(): return lax.ppermute(value, axis, [(i, i ^ mask) for i in range(size)])]
    pallas_call x0 -> x2, Pallas kernels: none -> 275 us  [the longest x1 174 us: finish(): pl.pallas_call(functools.partial(finish_kernel, rows_y), name='finish', o...]
    ppermute x60 -> x11, starting transfers between devices: 57.3 us -> 7.17 us  [swap(): return lax.ppermute(value, axis, [(i, i ^ mask) for i in range(size)])]
    dot_general x6 -> x3, matrix products: 43.1 us -> 11 us  [transposed(): lax.dot_general(left_side, right_side, (((0,), (0,)), ((), ())), preferre...]
    convert_element_type x4 -> x1, local copies, waits for them, and re-layouts: 32 us -> 0.22 us  [local(): grad_mixed = canonical(against(grad_branch, full_output).astype(bf16))]
    convert_element_type x10 -> x1, other arithmetic: 21.9 us -> 1.91 us  [local(): summed = summed.astype(f32)]
    concatenate x5 -> x2, local copies, waits for them, and re-layouts: 5.69 us -> 19.6 us  [the longest x1 19.5 us: local(): jnp.concatenate([part_qkv.astype(bf16), part_output.astype(bf16), part_sm...]
    another operation x27 -> x4, other arithmetic: 12 us -> 0.3 us  [the longest x5 4.12 us: local(): all_dy = jnp.stack(dy_groups)]
  transfers between devices with their start and end apart: 60 -> 11, of which waited for: 29 -> 5; matrix products, arithmetic and copies ran while one was open for 17% -> 5% of each run, Pallas kernels for 0% -> 0%
where the time goes in v2:
time: 579 us; the launch traced here: 572 us
  Pallas kernels  397 us (69%)
  local copies, waits for them, and re-layouts  61.9 us (11%)
  matrix products  45.8 us (8%)
  waiting for transfers between devices  35.3 us (6%)
  other arithmetic  23.9 us (4%)
  starting transfers between devices  7.17 us (1%)
    pallas_call x1, Pallas kernels, finish(): pl.pallas_call(functools.partial(finish_kernel, rows_y), name='finish', o...  174 us
    pallas_call x1, Pallas kernels, moe(): pl.pallas_call(functools.partial(moe_kernel, rows_y), name='moe', out_sha...  121 us
    pallas_call x1, Pallas kernels, gather(): pl.pallas_call(functools.partial(gather_kernel, rows_y, exclusive), name=...  101 us
    ppermute x11, waiting for transfers between devices, swap(): return lax.ppermute(value, axis, [(i, i ^ mask) for i in range(size)])  35.3 us
    concatenate x1, local copies, waits for them, and re-layouts, local(): jnp.concatenate([part_qkv.astype(bf16), part_output.astype(bf16), part_sm...  19.5 us
    dot_general x7, matrix products, dot(): return jnp.dot(left_side, right_side, preferred_element_type=f32)  19.5 us
    unnamed x124, local copies, waits for them, and re-layouts  17.3 us
  transfers between devices with their start and end apart: 11, of which 5 were waited for; matrix products, arithmetic and copies ran while one was open for 5% of the time, Pallas kernels for 0%

profile of v2, /device:TPU:0, one launch (start us, length us, event | category | flops | bytes accessed | tf_op | source)
XLA Modules:
  0.0 572.4 jit_solution(5902817224308012379)
XLA Ops:
  9.3 101.1 %gather.1 = (bf16[8,192,2560]{2,1,0:T(8,128)(2,1)}, bf16[8,192,1536]{2,1,0:T(8,128)(2,1)}, bf16[8,192,128]{2,1,0:T(8,128)(2,1)}, bf16[4,512,1664]{2,1,0:T(8,128)(2,1)}) custom-call(bf16[192,2560]{1,0:T(8,128)(2,1)} %pad_maximum_fusion.refs_0_, bf16[192,1536]{1,0:T(8,128)(2,1)} %refs_1_.1, bf16[192,128]{1,0:T(8,128)(2,1)} %maximum_maximum_fusion.refs_2_, ...), custom_call_target="tpu_custom_call" | custom-call | tf_op jit(solution)/shard_map/gather/pallas_call | solution.py:397
  112.6 4.5 fusion.39
  124.4 3.2 multiply_reduce_fusion.2
  127.7 4.3 constant_dynamic-slice_fusion
  132.9 121.5 %moe.1 = (bf16[4,512,1536]{2,1,0:T(8,128)(2,1)}, bf16[4,512,2560]{2,1,0:T(8,128)(2,1)}, bf16[4,512,1280]{2,1,0:T(8,128)(2,1)}, f32[128,1664]{1,0:T(8,128)}) custom-call(bf16[128,1536]{1,0:T(8,128)(2,1)} %multiply_convert_fusion.normed_ref, bf16[4,512,1664]{2,1,0:T(8,128)(2,1)} %get-tuple-element.25.dy_hbm, bf16[10,1536,1024]{2,1,0:T(8,128)(2,1)} %gate_up_hbm.1, ...), custom_call_target="tpu_custom_call" | custom-call | tf_op jit(solution)/shard_map/moe/pallas_call | solution.py:654
  254.4 4.8 convolution_convert_fusion.2
  260.7 2.2 convolution_convert_fusion.3
  264.8 2.2 convolution_convert_fusion.4
  268.4 2.2 convolution_convert_fusion.5
  280.2 2.3 collective-permute-start.8
  289.2 3.3 collective-permute-done.8
  293.2 16.1 %collective-permute-done.3 = bf16[128,1536]{1,0:T(8,128)(2,1)S(1)} collective-permute-done((bf16[128,1536]{1,0:T(8,128)(2,1)S(1)}, bf16[128,1536]{1,0:T(8,128)(2,1)S(1)}, u32[]{:S(2)}, u32[]{:S(2)}) %collective-permute-start.3) | collective-permute-done | bytes 393248 | tf_op jit(solution)/shard_map/ppermute | solution.py:61
  310.0 2.3 collective-permute-done.9
  313.5 3.0 multiply_reduce_fusion
  319.4 10.0 %collective-permute-done.4 = bf16[128,1536]{1,0:T(8,128)(2,1)} collective-permute-done((bf16[128,1536]{1,0:T(8,128)(2,1)S(1)}, bf16[128,1536]{1,0:T(8,128)(2,1)}, u32[]{:S(2)}, u32[]{:S(2)}) %collective-permute-start.4) | collective-permute-done | bytes 393248 | tf_op jit(solution)/shard_map/ppermute | solution.py:61
  329.4 3.6 collective-permute-done.10
  333.0 2.8 multiply_add_fusion
  335.8 4.3 convolution_convert_fusion.6
  344.2 3.6 convolution_convert_fusion.1
  348.5 3.8 fusion.27
  352.2 5.6 convolution_convert_fusion
  358.6 19.5 %concatenate.56.att_hbm = bf16[8,192,4224]{2,1,0:T(8,128)(2,1)} concatenate(bf16[8,192,2560]{2,1,0:T(8,128)(2,1)} %bitcast.103, bf16[8,192,1536]{2,1,0:T(8,128)(2,1)} %bitcast.104, bf16[8,192,40]{2,1,0:T(8,128)(2,1)S(1)} %bitcast.124, bf16[8,192,1]{2,1,0:T(8,128)(2,1)S(1)} %convert_element_type.304, bf16[8,192,1]{2,1,0:T(8,128)(2,1)S(1)} %copy-done.21, ...), dimensions={2} | concatenate | bytes 25952256 | tf_op jit(solution)/shard_map/concatenate | solution.py:1347
  378.1 174.0 %finish.1 = (f32[10,192,1024]{2,1,0:T(8,128)}, f32[10,64,1536]{2,1,0:T(8,128)}, bf16[192,4224]{1,0:T(8,128)(2,1)}) custom-call(bf16[4,512,1536]{2,1,0:T(8,128)(2,1)} %get-tuple-element.28.rows_hbm, bf16[4,512,2560]{2,1,0:T(8,128)(2,1)} %get-tuple-element.29.grads_hbm, bf16[4,512,1280]{2,1,0:T(8,128)(2,1)} %get-tuple-element.26.acts_hbm, ...), custom_call_target="tpu_custom_call" | custom-call | tf_op jit(solution)/shard_map/finish/pallas_call | solution.py:1068
  562.1 8.1 %copy.119 = f32[10,192,1024]{2,1,0:T(8,128)} copy(f32[10,192,1024]{2,1,0:T(8,128)} %get-tuple-element.132) | data formatting | bytes 15728640
  (215 shorter events, 62.4 us)
Async XLA Ops:
  1.9 110.1 %copy-start.46 = (f32[128]{0:T(128)}, f32[128]{0:T(128)S(1)}, u32[]{:S(2)}) copy-start(f32[128]{0:T(128)S(1)} %add_rsqrt_fusion.1) | copy-start | bytes 1540
  8.6 104.1 %copy-start = (bf16[128,1536]{1,0:T(8,128)(2,1)S(1)}, bf16[128,1536]{1,0:T(8,128)(2,1)}, u32[]{:S(2)}) copy-start(bf16[128,1536]{1,0:T(8,128)(2,1)} %param.13) | copy-start | bytes 1179652
  112.0 20.0 %copy-start.40 = (f32[1536]{0:T(1024)}, f32[1536]{0:T(1024)S(1)}, u32[]{:S(2)}) copy-start(f32[1536]{0:T(1024)S(1)} %get-tuple-element.83) | copy-start | bytes 18436
  260.7 17.9 %collective-permute-start.7 = (bf16[256,1536]{1,0:T(8,128)(2,1)}, bf16[256,1536]{1,0:T(8,128)(2,1)}, u32[]{:S(2)}, u32[]{:S(2)}) collective-permute-start(bf16[256,1536]{1,0:T(8,128)(2,1)} %slice.196), channel_id=1, source_target_pairs={{0,1},{1,0},{2,3},{3,2},{4,5},{5,4},{6,7},{7,6},{8,9},{9,8},{10,11... | collective-permute-start | bytes 2359304 | tf_op jit(solution)/shard_map/ppermute | solution.py:61
  264.3 18.3 %collective-permute-start.5 = (bf16[256,1536]{1,0:T(8,128)(2,1)}, bf16[256,1536]{1,0:T(8,128)(2,1)}, u32[]{:S(2)}, u32[]{:S(2)}) collective-permute-start(bf16[256,1536]{1,0:T(8,128)(2,1)} %slice.192), channel_id=1, source_target_pairs={{0,1},{1,0},{2,3},{3,2},{4,5},{5,4},{6,7},{7,6},{8,9},{9,8},{10,11... | collective-permute-start | bytes 2359304 | tf_op jit(solution)/shard_map/ppermute | solution.py:61
  268.4 15.7 %collective-permute-start.2 = (bf16[256,1536]{1,0:T(8,128)(2,1)}, bf16[256,1536]{1,0:T(8,128)(2,1)}, u32[]{:S(2)}, u32[]{:S(2)}) collective-permute-start(bf16[256,1536]{1,0:T(8,128)(2,1)} %slice.188), channel_id=1, source_target_pairs={{0,1},{1,0},{2,3},{3,2},{4,5},{5,4},{6,7},{7,6},{8,9},{9,8},{10,11... | collective-permute-start | bytes 2359304 | tf_op jit(solution)/shard_map/ppermute | solution.py:61
  271.8 15.6 %collective-permute-start = (bf16[256,1536]{1,0:T(8,128)(2,1)S(1)}, bf16[256,1536]{1,0:T(8,128)(2,1)}, u32[]{:S(2)}, u32[]{:S(2)}) collective-permute-start(bf16[256,1536]{1,0:T(8,128)(2,1)S(1)} %slice.184), channel_id=1, source_target_pairs={{0,1},{1,0},{2,3},{3,2},{4,5},{5,4},{6,7},{7,6},{8,9},{9,8},{10,11... | collective-permute-start | bytes 2359304 | tf_op jit(solution)/shard_map/ppermute | solution.py:61
  280.2 12.2 %collective-permute-start.8 = (bf16[128,1536]{1,0:T(8,128)(2,1)S(1)}, bf16[128,1536]{1,0:T(8,128)(2,1)S(1)}, u32[]{:S(2)}, u32[]{:S(2)}) collective-permute-start(bf16[128,1536]{1,0:T(8,128)(2,1)S(1)} %slice.198), channel_id=1, source_target_pairs={{0,2},{1,3},{2,0},{3,1},{4,6},{5,7},{6,4},{7,5},{8,10},{9,11},{10,... | collective-permute-start | bytes 1179656 | tf_op jit(solution)/shard_map/ppermute | solution.py:61
  283.9 26.1 %collective-permute-start.6 = (bf16[128,1536]{1,0:T(8,128)(2,1)S(1)}, bf16[128,1536]{1,0:T(8,128)(2,1)S(1)}, u32[]{:S(2)}, u32[]{:S(2)}) collective-permute-start(bf16[128,1536]{1,0:T(8,128)(2,1)S(1)} %slice.194), channel_id=1, source_target_pairs={{0,2},{1,3},{2,0},{3,1},{4,6},{5,7},{6,4},{7,5},{8,10},{9,11},{10,... | collective-permute-start | bytes 1179656 | tf_op jit(solution)/shard_map/ppermute | solution.py:61
  285.6 23.7 %collective-permute-start.3 = (bf16[128,1536]{1,0:T(8,128)(2,1)S(1)}, bf16[128,1536]{1,0:T(8,128)(2,1)S(1)}, u32[]{:S(2)}, u32[]{:S(2)}) collective-permute-start(bf16[128,1536]{1,0:T(8,128)(2,1)S(1)} %slice.190), channel_id=1, source_target_pairs={{0,2},{1,3},{2,0},{3,1},{4,6},{5,7},{6,4},{7,5},{8,10},{9,11},{10,... | collective-permute-start | bytes 1179656 | tf_op jit(solution)/shard_map/ppermute | solution.py:61
  288.8 24.4 %copy-start.9 = (bf16[256,1536]{1,0:T(8,128)(2,1)}, bf16[256,1536]{1,0:T(8,128)(2,1)S(1)}, u32[]{:S(2)}) copy-start(bf16[256,1536]{1,0:T(8,128)(2,1)S(1)} %add_convert_fusion.3) | copy-start | bytes 2359300
  288.8 30.6 %collective-permute-start.1 = (bf16[128,1536]{1,0:T(8,128)(2,1)S(1)}, bf16[128,1536]{1,0:T(8,128)(2,1)}, u32[]{:S(2)}, u32[]{:S(2)}) collective-permute-start(bf16[128,1536]{1,0:T(8,128)(2,1)S(1)} %slice.186), channel_id=1, source_target_pairs={{0,2},{1,3},{2,0},{3,1},{4,6},{5,7},{6,4},{7,5},{8,10},{9,11},{10,... | collective-permute-start | bytes 1179656 | tf_op jit(solution)/shard_map/ppermute | solution.py:61
  292.6 20.9 %copy-start.28 = (f32[128,40]{1,0:T(8,128)S(1)}, f32[128,40]{1,0:T(8,128)}, u32[]{:S(2)}) copy-start(f32[128,40]{1,0:T(8,128)} %copy-done.27) | copy-start | bytes 61444
  292.6 20.9 %copy-start.37 = (pred[128,40]{1,0:T(32,128)(4,1)S(1)}, pred[128,40]{1,0:T(32,128)(4,1)}, u32[]{:S(2)}) copy-start(pred[128,40]{1,0:T(32,128)(4,1)} %copy-done.36) | copy-start | bytes 15364
  292.6 20.9 %copy-start.41 = (f32[1536]{0:T(1024)S(1)}, f32[1536]{0:T(1024)}, u32[]{:S(2)}) copy-start(f32[1536]{0:T(1024)} %copy-done.40) | copy-start | bytes 18436
  292.6 20.9 %copy-start.50 = (f32[128]{0:T(128)S(1)}, f32[128]{0:T(128)}, u32[]{:S(2)}) copy-start(f32[128]{0:T(128)} %copy-done.49) | copy-start | bytes 1540
  292.6 20.9 %copy-start.52 = (f32[128]{0:T(128)S(1)}, f32[128]{0:T(128)}, u32[]{:S(2)}) copy-start(f32[128]{0:T(128)} %copy-done.51) | copy-start | bytes 1540
  292.6 20.9 %copy-start.54 = (f32[128]{0:T(128)S(1)}, f32[128]{0:T(128)}, u32[]{:S(2)}) copy-start(f32[128]{0:T(128)} %copy-done.53) | copy-start | bytes 1540
  292.7 20.9 %copy-start.56 = (f32[128]{0:T(128)S(1)}, f32[128]{0:T(128)}, u32[]{:S(2)}) copy-start(f32[128]{0:T(128)} %copy-done.55) | copy-start | bytes 1540
  292.7 19.6 %collective-permute-start.9 = (bf16[128,1536]{1,0:T(8,128)(2,1)S(1)}, bf16[128,1536]{1,0:T(8,128)(2,1)S(1)}, u32[]{:S(2)}, u32[]{:S(2)}) collective-permute-start(bf16[128,1536]{1,0:T(8,128)(2,1)S(1)} %add_convert_fusion.6), channel_id=1, source_target_pairs={{0,16},{4,20},{8,24},{12,28},{16,0},{20,4},{24,8},{28,12},{1,17},{... | collective-permute-start | bytes 1179656 | tf_op jit(solution)/shard_map/ppermute | solution.py:61
  309.4 19.9 %collective-permute-start.4 = (bf16[128,1536]{1,0:T(8,128)(2,1)S(1)}, bf16[128,1536]{1,0:T(8,128)(2,1)}, u32[]{:S(2)}, u32[]{:S(2)}) collective-permute-start(bf16[128,1536]{1,0:T(8,128)(2,1)S(1)} %add_convert_fusion.8), channel_id=1, source_target_pairs={{0,16},{4,20},{8,24},{12,28},{16,0},{20,4},{24,8},{28,12},{1,17},{... | collective-permute-start | bytes 1179656 | tf_op jit(solution)/shard_map/ppermute | solution.py:61
  313.2 19.8 %copy-start.20 = (bf16[128,1536]{1,0:T(8,128)(2,1)S(1)}, bf16[128,1536]{1,0:T(8,128)(2,1)}, u32[]{:S(2)}) copy-start(bf16[128,1536]{1,0:T(8,128)(2,1)} %param.25) | copy-start | bytes 1179652
  313.2 19.7 %collective-permute-start.10 = (bf16[128,1536]{1,0:T(8,128)(2,1)}, bf16[128,1536]{1,0:T(8,128)(2,1)}, u32[]{:S(2)}, u32[]{:S(2)}) collective-permute-start(bf16[128,1536]{1,0:T(8,128)(2,1)} %add_convert_fusion.5), channel_id=1, source_target_pairs={{0,8},{4,12},{8,0},{12,4},{16,24},{20,28},{24,16},{28,20},{1,9},{5... | collective-permute-start | bytes 1179656 | tf_op jit(solution)/shard_map/ppermute | solution.py:61
  335.8 8.4 %copy-start.2 = (f32[128,1536]{1,0:T(8,128)}, f32[128,1536]{1,0:T(8,128)S(1)}, u32[]{:S(2)}) copy-start(f32[128,1536]{1,0:T(8,128)S(1)} %get-tuple-element.93) | copy-start | bytes 2359300
  (48 other events, 136.8 us)
